TPU v7x, 32 devices: a whole 2x2x4 slice. The times are simulated.
32 devices in a mesh: groups: 2 (over x), cols: 16 (over z, y, core).
Axes of the slice: x: 2, y: 2, z: 4, core: 2. Of those that a mesh axis runs over, the one named last changes fastest.
Arguments:
- upper_left: bfloat16 [76800, 1024], P(('groups', 'cols')), parts along dimension 0, may hold values from -0.25 to 0.25
- upper_right: bfloat16 [76800, 1024], P(('groups', 'cols')), parts along dimension 0, may hold values from -0.0390625 to 0.0390625
- lower_left: bfloat16 [76800, 1024], P(('groups', 'cols')), parts along dimension 0, may hold values from -0.0390625 to 0.0390625
- lower_right: bfloat16 [76800, 1024], P(('groups', 'cols')), parts along dimension 0, may hold values from -0.25 to 0.25
- sketch_right: bfloat16 [76800, 384], P(('groups', 'cols')), parts along dimension 0, may hold values from -6 to 6
- sketch_left: bfloat16 [76800, 384], P(('groups', 'cols')), parts along dimension 0, may hold values from -6 to 6
- pairing: int32 [32], P('groups'), parts along dimension 0, may hold values from 0 to 15, each once
Outputs:
- upper_panel: float32 [2048, 384], P(('groups', 'cols')), parts along dimension 0
- lower_panel: float32 [2048, 384], P(('groups', 'cols')), parts along dimension 0
There are 2 independent parts, one for each index of `groups`. A program takes and returns all parts, laid end to end along the dimension named above; each array names one. Nothing has to cross between parts.
Inputs may be any that keep to these rules, and one draw needn't show every extreme that they name: pairing names every index of the cols axis once.
All inputs are finite; a program needn't handle non-finite values.
Results may differ from a plain program's by a relative error of at most 0.0089.
Values may be sent and summed in bfloat16 or wider, within the bound.
A program may use at most 128 MiB of HBM per device.

v0:
```python
import jax
import jax.numpy as jnp
from jax import lax
from jax.sharding import PartitionSpec as P


def contract(first, second):
    return lax.dot_general(
        first, second, (((0,), (0,)), ((), ())), preferred_element_type=jnp.float32
    )


def contract_exact(first, second):
    return lax.dot_general(
        first,
        second,
        (((0,), (0,)), ((), ())),
        precision=lax.Precision.HIGHEST,
        preferred_element_type=jnp.float32,
    )


def back_solve(factor, values):
    return lax.linalg.triangular_solve(
        factor, values, left_side=False, lower=True, transpose_a=True
    )


def per_device(
    upper_left, upper_right, lower_left, lower_right, sketch_right, sketch_left, pairing
):
    col_count = lax.axis_size("cols")
    panel_cols = upper_left.shape[1]
    block_rows = panel_cols // col_count
    rank_cols = sketch_right.shape[1]
    half_rows = upper_left.shape[0] * col_count
    columns = jnp.arange(panel_cols, dtype=jnp.int32)
    column_map = pairing[columns // block_rows] * block_rows + columns % block_rows
    aligned = jnp.take(lower_right, column_map, axis=1)

    def panel_sums(first, second, third, fourth):
        return lax.psum_scatter(
            jnp.concatenate([contract(first, second), contract(third, fourth)], axis=1),
            "cols",
            scatter_dimension=0,
            tiled=True,
        ).astype(jnp.bfloat16)

    def panel_apply(shares, first, third):
        gathered = lax.all_gather(shares, "cols", axis=0, tiled=True)
        return (
            jnp.dot(first, gathered[:, :rank_cols], preferred_element_type=jnp.float32),
            jnp.dot(third, gathered[:, rank_cols:], preferred_element_type=jnp.float32),
        )

    first_shares = panel_sums(lower_left, sketch_right, upper_left, sketch_left)
    second_right, second_left = panel_apply(first_shares, aligned, upper_right)
    third_shares = panel_sums(
        upper_right, second_right.astype(jnp.bfloat16), aligned, second_left.astype(jnp.bfloat16)
    )
    range_right, range_left = panel_apply(third_shares, upper_left, lower_left)
    upper_wide = upper_left.astype(jnp.float32)
    lower_wide = lower_left.astype(jnp.float32)
    shares = lax.psum_scatter(
        jnp.concatenate(
            [contract_exact(upper_wide, range_right), contract_exact(lower_wide, range_left)],
            axis=1,
        ),
        "cols",
        scatter_dimension=0,
        tiled=True,
    )
    grams = lax.psum(
        (contract_exact(range_right, range_right), contract_exact(range_left, range_left)), "cols"
    )
    factor_right = jnp.linalg.cholesky(grams[0] / half_rows)
    factor_left = jnp.linalg.cholesky(grams[1] / half_rows)
    upper_panel = back_solve(factor_right, shares[:, :rank_cols])
    lower_panel = back_solve(factor_left, shares[:, rank_cols:])
    return (upper_panel, lower_panel)


def solution(mesh):
    placed = (
        P(("groups", "cols"), None),
        P(("groups", "cols"), None),
        P(("groups", "cols"), None),
        P(("groups", "cols"), None),
        P(("groups", "cols"), None),
        P(("groups", "cols"), None),
        P("groups"),
    )
    return jax.shard_map(
        per_device,
        mesh=mesh,
        in_specs=placed,
        out_specs=(P(("groups", "cols"), None), P(("groups", "cols"), None)),
        check_vma=False,
    )
```

profile of v0, /device:TPU:29, one launch (start us, length us, event | category | flops | bytes accessed | tf_op | source)
XLA Modules:
  0.0 602.1 jit_solution(566067654061270966)
XLA Ops:
  21.5 63.8 %reduce-scatter.10.cloned.1.call-done = f32[64,768]{1,0:T(8,128)} async-done(((f32[1024,768]{1,0:T(8,128)}), f32[64,768]{1,0:T(8,128)}) %reduce-scatter.10.cloned.1.call-update) | async-done | bytes 196624 | tf_op jit(solution)/shard_map/reduce_scatter | solution.py:42
  105.5 13.2 %gather_fusion = bf16[1024,2400]{1,0:T(8,128)(2,1)} fusion(bf16[2400,1024]{0,1:T(8,128)(2,1)} %copy.28, s32[1024]{0:T(1024)S(1)} %broadcast_clamp_fusion), kind=kCustom, calls=%fused_computation | custom fusion | bytes 9834496 | tf_op jit(solution)/shard_map/jit(_take)/gather | solution.py:39
  118.8 9.9 %all-gather.3.cloned.1.call-done = bf16[1024,768]{1,0:T(8,128)(2,1)} async-done(((bf16[64,768]{1,0:T(8,128)(2,1)}), bf16[1024,768]{1,0:T(8,128)(2,1)}) %all-gather.3.cloned.1.call-update) | async-done | bytes 1572880 | tf_op jit(solution)/shard_map/all_gather | solution.py:50
  128.6 9.0 %convolution_bitcast_fusion.2 = f32[1024,384]{0,1:T(8,128)S(1)} fusion(bf16[2400,1024]{1,0:T(8,128)(2,1)} %param.11, bf16[1024,2400]{1,0:T(8,128)(2,1)} %gather_fusion, pred[1024]{0:T(1024)(128)(4,1)S(1)} %get-tuple-element.38, bf16[1024,768]{1,0:T(8,128)(2,1)} %all-gather.3.cloned.1.call-done), kind=kOutput, calls=%fused_computation.14 | convolution fusion | flops 3778252800 | bytes 12256256 | tf_op jit(solution)/shard_map/dot_general | solution.py:8
  137.7 8.8 %fusion = f32[1024,384]{0,1:T(8,128)S(1)} fusion(bf16[1024,2400]{1,0:T(8,128)(2,1)} %gather_fusion, pred[1024]{0:T(1024)(128)(4,1)S(1)} %get-tuple-element.38, bf16[2400,1024]{1,0:T(8,128)(2,1)} %param.11, bf16[1024,768]{1,0:T(8,128)(2,1)} %all-gather.3.cloned.1.call-done), kind=kOutput, calls=%fused_computation.11 | convolution fusion | flops 3778252800 | bytes 12256256 | tf_op jit(solution)/shard_map/dot_general | solution.py:8
  152.4 63.0 %reduce-scatter.12.cloned.1.call-done = f32[64,768]{1,0:T(8,128)} async-done(((f32[1024,768]{1,0:T(8,128)}), f32[64,768]{1,0:T(8,128)}) %reduce-scatter.12.cloned.1.call-update) | async-done | bytes 196624 | tf_op jit(solution)/shard_map/reduce_scatter | solution.py:42
  217.0 41.5 %all-gather.5.cloned.1.call-done = bf16[1024,768]{1,0:T(8,128)(2,1)} async-done(((bf16[64,768]{1,0:T(8,128)(2,1)}), bf16[1024,768]{1,0:T(8,128)(2,1)}) %all-gather.5.cloned.1.call-update) | async-done | bytes 1572880 | tf_op jit(solution)/shard_map/all_gather | solution.py:50
  271.5 8.7 %convolution_bitcast_fusion = f32[1024,384]{0,1:T(8,128)S(1)} fusion(f32[384,2400]{0,1:T(8,128)S(1)} %fusion.1, bf16[2400,1024]{1,0:T(8,128)(2,1)} %param.12), kind=kOutput, calls=%fused_computation.12 | convolution fusion | flops 11324620800 | bytes 10174464 | tf_op jit(solution)/shard_map/dot_general | solution.py:14
  284.7 8.1 %fusion.58 = f32[384,384]{0,1:T(8,128)} fusion(f32[384,2400]{0,1:T(8,128)S(1)} %fusion.3), kind=kOutput, calls=%fused_computation.147 | convolution fusion | flops 4246732800 | bytes 4276224 | tf_op jit(solution)/shard_map/dot_general | solution.py:14
  292.9 8.9 %convolution_bitcast_fusion.1 = f32[1024,384]{0,1:T(8,128)S(1)} fusion(f32[384,2400]{0,1:T(8,128)} %copy-done.2, bf16[2400,1024]{1,0:T(8,128)(2,1)} %param.10), kind=kOutput, calls=%fused_computation.13 | convolution fusion | flops 11324620800 | bytes 10174464 | tf_op jit(solution)/shard_map/dot_general | solution.py:14
  307.6 76.8 %all-reduce.4.cloned.1.call-done = (f32[384,384]{0,1:T(8,128)}, f32[384,384]{0,1:T(8,128)}) async-done(((f32[384,384]{0,1:T(8,128)}, f32[384,384]{0,1:T(8,128)}), (f32[384,384]{0,1:T(8,128)}, f32[384,384]{0,1:T(8,128)})) %all-reduce.4.cloned.1.call-update) | async-done | bytes 1179664 | tf_op jit(solution)/shard_map/psum | solution.py:73
  388.3 11.7 %cholesky.261 = f32[128,128]{1,0:T(8,128)S(1)} custom-call(f32[128,128]{1,0:T(8,128)S(1)} %cholesky.318), custom_call_target="Cholesky" | custom-call | tf_op jit(solution)/shard_map/jit(cholesky)/cholesky | solution.py:77
  400.1 9.8 %custom-call.23 = f32[1,128,128]{1,2,0:T(8,128)S(1)} custom-call(f32[1,128,128]{2,1,0:T(8,128)S(1)} %get-tuple-element.50), custom_call_target="InvertDiagBlocksLowerTriangular" | custom-call | tf_op jit(solution)/shard_map/jit(cholesky)/cholesky | solution.py:77
  410.5 11.7 %cholesky.280 = f32[128,128]{1,0:T(8,128)S(1)} custom-call(f32[128,128]{1,0:T(8,128)S(1)} %cholesky.322), custom_call_target="Cholesky" | custom-call | tf_op jit(solution)/shard_map/jit(cholesky)/cholesky | solution.py:77
  423.5 10.2 %custom-call.24 = f32[1,128,128]{1,2,0:T(8,128)S(1)} custom-call(f32[1,128,128]{2,1,0:T(8,128)S(1)} %get-tuple-element.47), custom_call_target="InvertDiagBlocksLowerTriangular" | custom-call | tf_op jit(solution)/shard_map/jit(cholesky)/cholesky | solution.py:77
  434.2 11.7 %cholesky.299 = f32[128,128]{1,0:T(8,128)S(1)} custom-call(f32[128,128]{1,0:T(8,128)S(1)} %convolution_subtract_fusion.2), custom_call_target="Cholesky" | custom-call | tf_op jit(solution)/shard_map/jit(cholesky)/cholesky | solution.py:77
  454.6 29.7 %custom-call.25 = f32[3,128,128]{1,2,0:T(8,128)S(1)} custom-call(f32[3,128,128]{2,1,0:T(8,128)S(1)} %get-tuple-element.19), custom_call_target="InvertDiagBlocksLowerTriangular" | custom-call | tf_op jit(solution)/shard_map/triangular_solve/custom-call.2 | solution.py:24
  485.1 11.7 %cholesky.208 = f32[128,128]{1,0:T(8,128)S(1)} custom-call(f32[128,128]{1,0:T(8,128)S(1)} %cholesky.310), custom_call_target="Cholesky" | custom-call | tf_op jit(solution)/shard_map/jit(cholesky)/cholesky | solution.py:76
  496.9 9.8 %custom-call.20 = f32[1,128,128]{1,2,0:T(8,128)S(1)} custom-call(f32[1,128,128]{2,1,0:T(8,128)S(1)} %get-tuple-element.57), custom_call_target="InvertDiagBlocksLowerTriangular" | custom-call | tf_op jit(solution)/shard_map/jit(cholesky)/cholesky | solution.py:76
  509.1 11.7 %cholesky.227 = f32[128,128]{1,0:T(8,128)S(1)} custom-call(f32[128,128]{1,0:T(8,128)S(1)} %cholesky.314), custom_call_target="Cholesky" | custom-call | tf_op jit(solution)/shard_map/jit(cholesky)/cholesky | solution.py:76
  520.9 10.0 %custom-call.21 = f32[1,128,128]{1,2,0:T(8,128)S(1)} custom-call(f32[1,128,128]{2,1,0:T(8,128)S(1)} %get-tuple-element.54), custom_call_target="InvertDiagBlocksLowerTriangular" | custom-call | tf_op jit(solution)/shard_map/jit(cholesky)/cholesky | solution.py:76
  532.2 11.7 %cholesky.246 = f32[128,128]{1,0:T(8,128)S(1)} custom-call(f32[128,128]{1,0:T(8,128)S(1)} %convolution_subtract_fusion.3), custom_call_target="Cholesky" | custom-call | tf_op jit(solution)/shard_map/jit(cholesky)/cholesky | solution.py:76
  548.6 8.7 %while.4 = (s32[]{:T(128)}, f32[384,384]{1,0:T(8,128)}, s32[3,2]{0,1:T(2,128)S(1)}, f32[3,128,128]{2,1,0:T(8,128)S(1)}, s32[]{:T(128)}) while((s32[]{:T(128)}, f32[384,384]{1,0:T(8,128)}, s32[3,2]{0,1:T(2,128)S(1)}, f32[3,128,128]{2,1,0:T(8,128)S(1)}, s32[]{:T(128)}) %tuple.86), condition=%wide.while_cond, body=%wide.while_body.sunk | while | flops 2 | bytes 131181 | solution.py:24
  557.3 29.5 %custom-call.22 = f32[3,128,128]{1,2,0:T(8,128)S(1)} custom-call(f32[3,128,128]{2,1,0:T(8,128)S(1)} %get-tuple-element.18), custom_call_target="InvertDiagBlocksLowerTriangular" | custom-call | tf_op jit(solution)/shard_map/triangular_solve/custom-call.2 | solution.py:24
  (132 shorter events, 108.5 us)
Async XLA Ops:
  7.2 1.5 copy-start
  7.2 78.0 %reduce-scatter.10.cloned.1.call-start = ((), (), s32[]{:S(2)}) async-start(), calls=%async_computation.5 | async-start | bytes 3342336 | tf_op jit(solution)/shard_map/reduce_scatter | solution.py:42
  8.7 4.8 copy-start.6
  8.7 4.8 copy-start.7
  21.4 107.2 %all-gather.3.cloned.1.call-start = ((), (), s32[]{:S(2)}) async-start(), calls=%async_computation.3 | async-start | bytes 1671168 | tf_op jit(solution)/shard_map/all_gather | solution.py:50
  86.8 8.0 %copy-start.5 = (s32[16]{0:T(128)S(1)}, s32[16]{0:T(128)}, u32[]{:S(2)}) copy-start(s32[16]{0:T(128)} %param.16) | copy-start | bytes 196
  86.8 128.6 %reduce-scatter.12.cloned.1.call-start = ((), (), s32[]{:S(2)}) async-start(), calls=%async_computation.6 | async-start | bytes 3342336 | tf_op jit(solution)/shard_map/reduce_scatter | solution.py:42
  152.0 106.6 %all-gather.5.cloned.1.call-start = ((), (), s32[]{:S(2)}) async-start(), calls=%async_computation.4 | async-start | bytes 1671168 | tf_op jit(solution)/shard_map/all_gather | solution.py:50
  217.0 167.5 %all-reduce.4.cloned.1.call-start = ((), (), s32[]{:S(2)}) async-start(), calls=%async_computation.8 | async-start | bytes 2359296 | tf_op jit(solution)/shard_map/psum | solution.py:73
  263.4 16.8 %slice-start = ((s8[4915200]{0:T(1024)(128)(4,1)}), s8[4194304]{0:T(1024)(128)(4,1)S(1)}, s32[]{:S(2)}) async-start(s8[4915200]{0:T(1024)(128)(4,1)} %bitcast.131), calls=%async_computation.9 | async-start | bytes 8388608
  271.5 8.7 %slice-start.1 = ((s8[4915200]{0:T(1024)(128)(4,1)}), s8[720896]{0:T(1024)(128)(4,1)S(1)}, s32[]{:S(2)}) async-start(s8[4915200]{0:T(1024)(128)(4,1)} %bitcast.131), calls=%async_computation.10 | async-start | bytes 1441792
  271.5 8.7 %copy-start.8 = (bf16[1024,768]{1,0:T(8,128)(2,1)S(1)}, bf16[1024,768]{1,0:T(8,128)(2,1)}, u32[]{:S(2)}) copy-start(bf16[1024,768]{1,0:T(8,128)(2,1)} %all-gather.5.cloned.1.call-done) | copy-start | bytes 4718596
  282.9 1.8 copy-start.2
  292.9 293.9 %reduce-scatter.14.cloned.1.call-start = ((), (), s32[]{:S(2)}) async-start(), calls=%async_computation.7 | async-start | bytes 3342336 | tf_op jit(solution)/shard_map/reduce_scatter | solution.py:64
  384.5 2.8 copy-start.3
  384.5 2.8 copy-start.4
  454.6 140.4 %copy-start.1 = (bf16[2400,384]{1,0:T(8,128)(2,1)S(1)}, bf16[2400,384]{1,0:T(8,128)(2,1)}, u32[]{:S(2)}) copy-start(bf16[2400,384]{1,0:T(8,128)(2,1)} %param.14) | copy-start | bytes 5529604
Sparse Core Ops, SparseCore 0:
  21.5 63.6 reduce-scatter.9
  88.1 40.5 all-gather.2
  152.1 63.2 reduce-scatter.11
  218.1 40.4 all-gather.4
  293.0 91.4 all-reduce.3
  388.1 64.9 reduce-scatter.13
where the time goes:
time: 612 us; the launch traced here: 602 us
  waiting for transfers between devices  255 us (42%)
  other arithmetic  198 us (32%)
  matrix products  77.7 us (13%)
  local copies, waits for them, and re-layouts  51.5 us (8%)
  between operations  18.6 us (3%)
    reduce_scatter x2, waiting for transfers between devices, panel_sums(): lax.psum_scatter(jnp.concatenate([contract(first, second), contract(third...  127 us
    psum x1, waiting for transfers between devices, per_device(): lax.psum((contract_exact(range_right, range_right), contract_exact(range_...  76.8 us
    another operation x7, other arithmetic, back_solve(): lax.linalg.triangular_solve(factor, values, left_side=False, lower=True,...  61.4 us
    another operation x11, other arithmetic, per_device(): factor_left = jnp.linalg.cholesky(grams[1] / half_rows)  57.2 us
    another operation x11, other arithmetic, per_device(): factor_right = jnp.linalg.cholesky(grams[0] / half_rows)  56.9 us
    all_gather x2, waiting for transfers between devices, panel_apply(): gathered = lax.all_gather(shares, 'cols', axis=0, tiled=True)  51.4 us
    dot_general x4, matrix products, contract_exact(): lax.dot_general(first, second, (((0,), (0,)), ((), ())), precision=lax.Pr...  33.8 us
    dot_general x4, matrix products, contract(): lax.dot_general(first, second, (((0,), (0,)), ((), ())), preferred_elemen...  24.9 us
  transfers between devices with their start and end apart: 6, of which 5 were waited for; matrix products, arithmetic and copies ran while one was open for 41% of the time, Pallas kernels for 0%

commit v1 on v0

v1 whole, which is shorter than its diff:
```python
import functools

import jax
import jax.numpy as jnp
from jax import lax
from jax.experimental import pallas as pl
from jax.experimental.pallas import tpu as pltpu
from jax.sharding import PartitionSpec as P

BLOCK = 256
PIVOTS = 64
F32 = jnp.float32
BF16 = jnp.bfloat16


def contract(first, second):
    return lax.dot_general(
        first, second, (((0,), (0,)), ((), ())), preferred_element_type=F32
    )


def dot_exact(first, second, dims=((1,), (0,))):
    return lax.dot_general(
        first, second, (dims, ((), ())), precision=lax.Precision.HIGHEST, preferred_element_type=F32
    )


def upper_blocks(array):
    order = array.shape[1]
    return jnp.concatenate(
        [contract(array[:, k : k + BLOCK], array[:, k:]) for k in range(0, order, BLOCK)], axis=1
    )


def exchange(value, bit, count):
    return lax.ppermute(value, "cols", [(i, i ^ (1 << bit)) for i in range(count)])


def sum_rows(partial, bits, me, count):
    for bit in bits:
        half = partial.shape[0] // 2
        mine = (me >> bit) & 1
        kept = lax.dynamic_slice_in_dim(partial, mine * half, half, 0)
        sent = lax.dynamic_slice_in_dim(partial, (1 - mine) * half, half, 0).astype(BF16)
        partial = kept + exchange(sent, bit, count).astype(F32)
    share = partial.astype(BF16)
    for bit in reversed(bits):
        mine = (me >> bit) & 1
        other = exchange(share, bit, count)
        share = jnp.where(
            mine == 0,
            jnp.concatenate([share, other], axis=0),
            jnp.concatenate([other, share], axis=0),
        )
    return share


def inverse_factors(blocks):
    size = PIVOTS
    rows = size // 8
    eye = (
        lax.broadcasted_iota(jnp.int32, (size, size), 0)
        == lax.broadcasted_iota(jnp.int32, (size, size), 1)
    ).astype(F32)
    sub = lax.broadcasted_iota(jnp.int32, (8, 2 * size), 0)
    tables = []
    for block in blocks:
        joined = jnp.concatenate([block, eye], axis=1)
        tables.append([joined[8 * c : 8 * c + 8] for c in range(rows)])
    for j in range(size):
        c0, r0 = j // 8, j % 8
        for t in tables:
            row = jnp.broadcast_to(t[c0][r0 : r0 + 1, :], (8, 2 * size))
            inv = 1.0 / jnp.broadcast_to(row[:, j : j + 1], (8, 2 * size))
            scaled = row * inv
            for c in range(c0, rows):
                col = jnp.broadcast_to(t[c][:, j : j + 1], (8, 2 * size))
                if c == c0:
                    col = jnp.where(sub > r0, col, 0.0)
                t[c] = t[c] - col * scaled
    out = []
    for t in tables:
        joined = jnp.concatenate(t, axis=0)
        diag = jnp.sum(joined[:, :size] * eye, axis=1, keepdims=True)
        out.append(joined[:, size:] * lax.rsqrt(diag))
    return out


def split3(value):
    high = value.astype(BF16)
    rest = value - high.astype(F32)
    mid = rest.astype(BF16)
    return high, mid, (rest - mid.astype(F32)).astype(BF16)


def tail_kernel(
    where_ref, pairing_ref, first_ref, middle_ref, upper_ref, lower_ref,
    out_up, out_low, moved, loose, gram_ref, table, *, half_rows, units
):
    order, rank2 = first_ref.shape
    rank = rank2 // 2
    unit = order // units
    share = out_up.shape[0]

    loose[...] = first_ref[:, :rank].astype(F32)

    @pl.loop(0, units)
    def _(i):
        moved[pl.ds(pl.multiple_of(pairing_ref[i] * unit, unit), unit), :] = loose[
            pl.ds(pl.multiple_of(i * unit, unit), unit), :
        ]

    third_right = jnp.dot(middle_ref[...], moved[...].astype(BF16), preferred_element_type=F32).astype(BF16)
    loose[...] = lax.dot_general(
        middle_ref[...], first_ref[:, rank:], (((0,), (0,)), ((), ())), preferred_element_type=F32
    )

    @pl.loop(0, units)
    def _(i):
        moved[pl.ds(pl.multiple_of(i * unit, unit), unit), :] = loose[
            pl.ds(pl.multiple_of(pairing_ref[i] * unit, unit), unit), :
        ]

    thirds = (third_right, moved[...].astype(BF16))
    for s, (third, square_ref) in enumerate(zip(thirds, (upper_ref, lower_ref))):
        base = 0
        parts = [None] * (order // BLOCK)
        for k in range(order // BLOCK):
            width = order - k * BLOCK
            strip = square_ref[:, base : base + width]
            base += width
            term = jnp.dot(strip, third[k * BLOCK :], preferred_element_type=F32)
            parts[k] = term if parts[k] is None else parts[k] + term
            if width > BLOCK:
                below = lax.dot_general(
                    strip[:, BLOCK:],
                    third[k * BLOCK : (k + 1) * BLOCK],
                    (((0,), (0,)), ((), ())),
                    preferred_element_type=F32,
                )
                for m in range(k + 1, order // BLOCK):
                    piece = below[(m - k - 1) * BLOCK : (m - k) * BLOCK]
                    parts[m] = piece if parts[m] is None else parts[m] + piece
        for k in range(order // BLOCK):
            table[s, k * BLOCK : (k + 1) * BLOCK, :] = parts[k]
        product = table[s]
        gram = sum(contract(third, piece) for piece in split3(product)) * (1.0 / half_rows)
        gram_ref[s, :, :rank] = gram
        gram_ref[s, :, rank:] = (
            lax.broadcasted_iota(jnp.int32, (rank, rank), 0)
            == lax.broadcasted_iota(jnp.int32, (rank, rank), 1)
        ).astype(F32)

    @pl.loop(0, rank // PIVOTS)
    def _(k):
        at = pl.multiple_of(k * PIVOTS, PIVOTS)
        rows = [gram_ref[s, pl.ds(at, PIVOTS), :] for s in range(2)]
        turned = [pltpu.roll(r[:, :rank], rank - at, 1)[:, :PIVOTS] for r in rows]
        inverses = inverse_factors(turned)
        beyond = lax.broadcasted_iota(jnp.int32, (PIVOTS, rank), 1) >= at + PIVOTS
        for s in range(2):
            done = dot_exact(inverses[s], rows[s])
            ahead = jnp.where(beyond, done[:, :rank], 0.0)
            gram_ref[s, :, :] = gram_ref[s, :, :] - dot_exact(ahead, done, ((0,), (0,)))
            gram_ref[s, pl.ds(at, PIVOTS), :] = done

    at = pl.multiple_of(where_ref[0] * share, share)
    for s, out in enumerate((out_up, out_low)):
        out[...] = dot_exact(
            table[s, pl.ds(at, share), :], gram_ref[s, :, rank:], ((1,), (1,))
        )


def tail(me, pairing, first, middle, upper, lower, half_rows, count):
    order = first.shape[0]
    rank = first.shape[1] // 2
    share = jax.ShapeDtypeStruct((order // count, rank), F32)
    smem = pl.BlockSpec(memory_space=pltpu.SMEM)
    vmem = pl.BlockSpec(memory_space=pltpu.VMEM)
    return pl.pallas_call(
        functools.partial(tail_kernel, half_rows=half_rows, units=count),
        out_shape=(share, share),
        in_specs=[smem, smem, vmem, vmem, vmem, vmem],
        out_specs=(vmem, vmem),
        scratch_shapes=[
            pltpu.VMEM((order, rank), F32),
            pltpu.VMEM((order, rank), F32),
            pltpu.VMEM((2, rank, 2 * rank), F32),
            pltpu.VMEM((2, order, rank), F32),
        ],
        compiler_params=pltpu.CompilerParams(vmem_limit_bytes=48 * 2**20),
    )(me[None], pairing, first, middle, upper, lower)


def per_device(
    upper_left, upper_right, lower_left, lower_right, sketch_right, sketch_left, pairing
):
    count = lax.axis_size("cols")
    me = lax.axis_index("cols").astype(jnp.int32)
    half_rows = upper_left.shape[0] * count
    bits = list(range(count.bit_length() - 1))
    near_first = bits
    far_first = bits[:1] + bits[2:] + bits[1:2]
    middle = sum_rows(contract(upper_right, lower_right), near_first, me, count)
    first = sum_rows(
        jnp.concatenate(
            [contract(lower_left, sketch_right), contract(upper_left, sketch_left)], axis=1
        ),
        far_first, me, count,
    )
    upper = sum_rows(upper_blocks(upper_left), near_first, me, count)
    lower = sum_rows(upper_blocks(lower_left), far_first, me, count)
    return tail(me, pairing, first, middle, upper, lower, half_rows, count)


def solution(mesh):
    rows = P(("groups", "cols"), None)
    return jax.shard_map(
        per_device,
        mesh=mesh,
        in_specs=(rows,) * 6 + (P("groups"),),
        out_specs=(rows, rows),
        check_vma=False,
    )
```

time: 612 us -> 244 us (0.40); the launches traced: 602 us -> 242 us
  other arithmetic: 198 us -> 19.8 us
  waiting for transfers between devices: 255 us -> 78.8 us
  Pallas kernels: 0 us -> 78.6 us
  local copies, waits for them, and re-layouts: 51.5 us -> 7.21 us
  matrix products: 77.7 us -> 33.8 us
  starting transfers between devices: 0.83 us -> 22.6 us
  between operations: 18.6 us -> 1.27 us
    another operation x29 -> x0, other arithmetic: 175 us -> none  [the longest x7 61.4 us: back_solve(): lax.linalg.triangular_solve(factor, values, left_side=False, lower=True,...]
    reduce_scatter x3 -> x0, waiting for transfers between devices: 127 us -> none  [the longest x2 127 us: panel_sums(): lax.psum_scatter(jnp.concatenate([contract(first, second), contract(third...]
    ppermute x0 -> x32, waiting for transfers between devices: none -> 78.8 us  [exchange(): lax.ppermute(value, 'cols', [(i, i ^ 1 << bit) for i in range(count)])]
    pallas_call x0 -> x1, Pallas kernels: none -> 78.6 us  [tail(): pl.pallas_call(functools.partial(tail_kernel, half_rows=half_rows, units=...]
    psum x1 -> x0, waiting for transfers between devices: 76.8 us -> none  [per_device(): lax.psum((contract_exact(range_right, range_right), contract_exact(range_...]
    all_gather x2 -> x0, waiting for transfers between devices: 51.4 us -> none  [panel_apply(): gathered = lax.all_gather(shares, 'cols', axis=0, tiled=True)]
    dot_general x6 -> x0, matrix products: 41.2 us -> none  [the longest x4 33.8 us: contract_exact(): lax.dot_general(first, second, (((0,), (0,)), ((), ())), precision=lax.Pr...]
    ppermute x0 -> x32, starting transfers between devices: none -> 22.6 us  [exchange(): lax.ppermute(value, 'cols', [(i, i ^ 1 << bit) for i in range(count)])]
  transfers between devices with their start and end apart: 6 -> 32, of which waited for: 5 -> 13; matrix products, arithmetic and copies ran while one was open for 41% -> 17% of each run, Pallas kernels for 0% -> 0%
where the time goes in v1:
time: 244 us; the launch traced here: 242 us
  waiting for transfers between devices  78.8 us (32%)
  Pallas kernels  78.6 us (32%)
  matrix products  33.8 us (14%)
  starting transfers between devices  22.6 us (9%)
  other arithmetic  19.8 us (8%)
  local copies, waits for them, and re-layouts  7.21 us (3%)
    ppermute x32, waiting for transfers between devices, exchange(): lax.ppermute(value, 'cols', [(i, i ^ 1 << bit) for i in range(count)])  78.8 us
    pallas_call x1, Pallas kernels, tail(): pl.pallas_call(functools.partial(tail_kernel, half_rows=half_rows, units=...  78.6 us
    dot_general x11, matrix products, contract(): lax.dot_general(first, second, (((0,), (0,)), ((), ())), preferred_elemen...  33.8 us
    ppermute x32, starting transfers between devices, exchange(): lax.ppermute(value, 'cols', [(i, i ^ 1 << bit) for i in range(count)])  22.6 us
    select_n x16, other arithmetic, sum_rows(): jnp.where(mine == 0, jnp.concatenate([share, other], axis=0), jnp.concate...  10.5 us
    add x12, other arithmetic, sum_rows(): partial = kept + exchange(sent, bit, count).astype(F32)  6.51 us
  transfers between devices with their start and end apart: 32, of which 13 were waited for; matrix products, arithmetic and copies ran while one was open for 17% of the time, Pallas kernels for 0%

profile of v1, /device:TPU:29, one launch (start us, length us, event | category | flops | bytes accessed | tf_op | source)
XLA Modules:
  0.0 242.1 jit_solution(11045232553155917730)
XLA Ops:
  0.7 4.5 %fusion.16 = f32[256,1024]{1,0:T(8,128)S(1)} fusion(bf16[2400,1024]{1,0:T(8,128)(2,1)} %param.9), kind=kOutput, calls=%fused_computation.32 | convolution fusion | flops 1258291200 | bytes 7192576 | tf_op jit(solution)/shard_map/dot_general | solution.py:17
  5.2 2.1 fusion
  12.5 5.1 %fusion.22 = f32[256,1024]{1,0:T(8,128)S(1)} fusion(bf16[2400,1024]{1,0:T(8,128)(2,1)} %param.7), kind=kOutput, calls=%fused_computation.38 | convolution fusion | flops 1258291200 | bytes 7192576 | tf_op jit(solution)/shard_map/dot_general | solution.py:17
  23.6 9.0 %fusion.26 = f32[1024,1024]{1,0:T(8,128)S(1)} fusion(bf16[2400,1024]{1,0:T(8,128)(2,1)} %param.8, bf16[2400,1024]{1,0:T(8,128)(2,1)} %param.10), kind=kOutput, calls=%fused_computation.78 | convolution fusion | flops 5033164800 | bytes 14024704 | tf_op jit(solution)/shard_map/dot_general | solution.py:17
  35.7 5.5 %fusion.24 = f32[1024,384]{1,0:T(8,128)S(1)} fusion(bf16[2400,1024]{1,0:T(8,128)(2,1)} %param.9, bf16[2400,384]{1,0:T(8,128)(2,1)S(1)} %copy-done), kind=kOutput, calls=%fused_computation.76 | convolution fusion | flops 1887436800 | bytes 8331264 | tf_op jit(solution)/shard_map/dot_general | solution.py:17
  41.2 2.8 %fusion.25 = f32[1024,384]{1,0:T(8,128)S(1)} fusion(bf16[2400,1024]{1,0:T(8,128)(2,1)S(1)} %bitcast.12, bf16[2400,384]{1,0:T(8,128)(2,1)S(1)} %copy-done.9), kind=kOutput, calls=%fused_computation.77 | convolution fusion | flops 1887436800 | bytes 8331264 | tf_op jit(solution)/shard_map/dot_general | solution.py:17
  52.1 4.8 %collective-permute-done.25 = bf16[64,2560]{1,0:T(8,128)(2,1)S(1)} collective-permute-done((bf16[64,2560]{1,0:T(8,128)(2,1)S(1)}, bf16[64,2560]{1,0:T(8,128)(2,1)S(1)}, u32[]{:S(2)}, u32[]{:S(2)}) %collective-permute-start.25) | collective-permute-done | bytes 327712 | tf_op jit(solution)/shard_map/ppermute | solution.py:36
  61.7 5.2 %collective-permute-done.26 = bf16[32,2560]{1,0:T(8,128)(2,1)S(1)} collective-permute-done((bf16[32,2560]{1,0:T(8,128)(2,1)S(1)}, bf16[32,2560]{1,0:T(8,128)(2,1)S(1)}, u32[]{:S(2)}, u32[]{:S(2)}) %collective-permute-start.26) | collective-permute-done | bytes 163872 | tf_op jit(solution)/shard_map/ppermute | solution.py:36
  67.2 5.2 %collective-permute-done.18 = bf16[32,2560]{1,0:T(8,128)(2,1)S(1)} collective-permute-done((bf16[32,2560]{1,0:T(8,128)(2,1)S(1)}, bf16[32,2560]{1,0:T(8,128)(2,1)S(1)}, u32[]{:S(2)}, u32[]{:S(2)}) %collective-permute-start.18) | collective-permute-done | bytes 163872 | tf_op jit(solution)/shard_map/ppermute | solution.py:36
  72.7 2.4 collective-permute-start.2
  75.6 10.8 %collective-permute-done.19 = bf16[16,2560]{1,0:T(8,128)(2,1)S(1)} collective-permute-done((bf16[16,2560]{1,0:T(8,128)(2,1)S(1)}, bf16[16,2560]{1,0:T(8,128)(2,1)S(1)}, u32[]{:S(2)}, u32[]{:S(2)}) %collective-permute-start.19) | collective-permute-done | bytes 81952 | tf_op jit(solution)/shard_map/ppermute | solution.py:36
  86.5 2.4 collective-permute-start.29
  88.9 6.0 %collective-permute-done.20 = bf16[16,2560]{1,0:T(8,128)(2,1)S(1)} collective-permute-done((bf16[16,2560]{1,0:T(8,128)(2,1)S(1)}, bf16[16,2560]{1,0:T(8,128)(2,1)S(1)}, u32[]{:S(2)}, u32[]{:S(2)}) %collective-permute-start.20) | collective-permute-done | bytes 81952 | tf_op jit(solution)/shard_map/ppermute | solution.py:36
  97.1 10.3 %collective-permute-done.10 = bf16[128,1024]{1,0:T(8,128)(2,1)S(1)} collective-permute-done((bf16[128,1024]{1,0:T(8,128)(2,1)S(1)}, bf16[128,1024]{1,0:T(8,128)(2,1)S(1)}, u32[]{:S(2)}, u32[]{:S(2)}) %collective-permute-start.10) | collective-permute-done | bytes 262176 | tf_op jit(solution)/shard_map/ppermute | solution.py:36
  107.9 9.2 %collective-permute-done.11 = bf16[64,1024]{1,0:T(8,128)(2,1)S(1)} collective-permute-done((bf16[64,1024]{1,0:T(8,128)(2,1)S(1)}, bf16[64,1024]{1,0:T(8,128)(2,1)S(1)}, u32[]{:S(2)}, u32[]{:S(2)}) %collective-permute-start.11) | collective-permute-done | bytes 131104 | tf_op jit(solution)/shard_map/ppermute | solution.py:36
  117.4 2.4 collective-permute-start.5
  119.8 2.9 %collective-permute-done.12 = bf16[64,1024]{1,0:T(8,128)(2,1)S(1)} collective-permute-done((bf16[64,1024]{1,0:T(8,128)(2,1)S(1)}, bf16[64,1024]{1,0:T(8,128)(2,1)S(1)}, u32[]{:S(2)}, u32[]{:S(2)}) %collective-permute-start.12) | collective-permute-done | bytes 131104 | tf_op jit(solution)/shard_map/ppermute | solution.py:36
  123.2 8.0 %collective-permute-done.5 = bf16[128,768]{1,0:T(8,128)(2,1)S(1)} collective-permute-done((bf16[128,768]{1,0:T(8,128)(2,1)S(1)}, bf16[128,768]{1,0:T(8,128)(2,1)S(1)}, u32[]{:S(2)}, u32[]{:S(2)}) %collective-permute-start.5) | collective-permute-done | bytes 196640 | tf_op jit(solution)/shard_map/ppermute | solution.py:36
  132.5 6.4 %collective-permute-done.13 = bf16[128,1024]{1,0:T(8,128)(2,1)S(1)} collective-permute-done((bf16[128,1024]{1,0:T(8,128)(2,1)S(1)}, bf16[128,1024]{1,0:T(8,128)(2,1)S(1)}, u32[]{:S(2)}, u32[]{:S(2)}) %collective-permute-start.13) | collective-permute-done | bytes 262176 | tf_op jit(solution)/shard_map/ppermute | solution.py:36
  139.4 2.4 collective-permute-start.31
  142.0 8.4 %collective-permute-done.14 = bf16[256,1024]{1,0:T(8,128)(2,1)S(1)} collective-permute-done((bf16[256,1024]{1,0:T(8,128)(2,1)S(1)}, bf16[256,1024]{1,0:T(8,128)(2,1)S(1)}, u32[]{:S(2)}, u32[]{:S(2)}) %collective-permute-start.14) | collective-permute-done | bytes 524320 | tf_op jit(solution)/shard_map/ppermute | solution.py:36
  150.9 3.0 %collective-permute-start.15 = (bf16[512,1024]{1,0:T(8,128)(2,1)S(1)}, bf16[512,1024]{1,0:T(8,128)(2,1)}, u32[]{:S(2)}, u32[]{:S(2)}) collective-permute-start(bf16[512,1024]{1,0:T(8,128)(2,1)S(1)} %maximum_select_fusion.4), channel_id=1, source_target_pairs={{0,1},{1,0},{2,3},{3,2},{4,5},{5,4},{6,7},{7,6},{8,9},{9,8},{10,11... | collective-permute-start | bytes 3145736 | tf_op jit(solution)/shard_map/ppermute | solution.py:36
  159.7 3.7 %maximum_select_fusion.middle_ref = bf16[1024,1024]{1,0:T(8,128)(2,1)} fusion(bf16[512,1024]{1,0:T(8,128)(2,1)} %collective-permute-done.15, bf16[512,1024]{1,0:T(8,128)(2,1)S(1)} %maximum_select_fusion.4, pred[]{:T(512)S(6)} %eq.8), kind=kLoop, calls=%fused_computation.14 | loop fusion | flops 9437184 | bytes 4194305 | tf_op jit(solution)/shard_map/jit(_where)/select_n | solution.py:50
  163.5 78.6 %shard_map.86 = (f32[64,384]{1,0:T(8,128)}, f32[64,384]{1,0:T(8,128)}) custom-call(s32[1]{0:T(128)} %bitcast.where_ref, s32[16]{0:T(128)S(1)} %copy-done.2, bf16[1024,768]{1,0:T(8,128)(2,1)S(1)} %maximum_select_fusion.1.first_ref, bf16[1024,1024]{1,0:T(8,128)(2,1)} %maximum_select_fusion.middle_ref, bf16[256,2560]{1,0:T(8,128)(2,1)S(1)} %maximum_select_fusion.2.upper_ref, ...), custom_call_target="tpu_custom_call" | custom-call | tf_op jit(solution)/shard_map/pallas_call | solution.py:180
  (132 shorter events, 39.6 us)
Async XLA Ops:
  11.8 33.9 %collective-permute-start.24 = (bf16[128,2560]{1,0:T(8,128)(2,1)}, bf16[128,2560]{1,0:T(8,128)(2,1)}, u32[]{:S(2)}, u32[]{:S(2)}) collective-permute-start(bf16[128,2560]{1,0:T(8,128)(2,1)} %dynamic-slice_convert_fusion.1), channel_id=1, source_target_pairs={{0,1},{1,0},{2,3},{3,2},{4,5},{5,4},{6,7},{7,6},{8,9},{9,8},{10,11... | collective-permute-start | bytes 1966088 | tf_op jit(solution)/shard_map/ppermute | solution.py:36
  23.1 24.8 %collective-permute-start.16 = (bf16[128,2560]{1,0:T(8,128)(2,1)}, bf16[128,2560]{1,0:T(8,128)(2,1)}, u32[]{:S(2)}, u32[]{:S(2)}) collective-permute-start(bf16[128,2560]{1,0:T(8,128)(2,1)} %dynamic-slice_convert_fusion.2), channel_id=1, source_target_pairs={{0,1},{1,0},{2,3},{3,2},{4,5},{5,4},{6,7},{7,6},{8,9},{9,8},{10,11... | collective-permute-start | bytes 1966088 | tf_op jit(solution)/shard_map/ppermute | solution.py:36
  35.6 24.0 %collective-permute-start.8 = (bf16[512,1024]{1,0:T(8,128)(2,1)}, bf16[512,1024]{1,0:T(8,128)(2,1)}, u32[]{:S(2)}, u32[]{:S(2)}) collective-permute-start(bf16[512,1024]{1,0:T(8,128)(2,1)} %dynamic-slice_convert_fusion), channel_id=1, source_target_pairs={{0,1},{1,0},{2,3},{3,2},{4,5},{5,4},{6,7},{7,6},{8,9},{9,8},{10,11... | collective-permute-start | bytes 3145736 | tf_op jit(solution)/shard_map/ppermute | solution.py:36
  51.0 21.6 %collective-permute-start.1 = (bf16[256,768]{1,0:T(8,128)(2,1)S(1)}, bf16[256,768]{1,0:T(8,128)(2,1)S(1)}, u32[]{:S(2)}, u32[]{:S(2)}) collective-permute-start(bf16[256,768]{1,0:T(8,128)(2,1)S(1)} %dynamic-slice_convert_fusion.4), channel_id=1, source_target_pairs={{0,4},{1,5},{2,6},{3,7},{4,0},{5,1},{6,2},{7,3},{8,12},{9,13},{10,... | collective-permute-start | bytes 1179656 | tf_op jit(solution)/shard_map/ppermute | solution.py:36
  57.1 9.8 %collective-permute-start.26 = (bf16[32,2560]{1,0:T(8,128)(2,1)S(1)}, bf16[32,2560]{1,0:T(8,128)(2,1)S(1)}, u32[]{:S(2)}, u32[]{:S(2)}) collective-permute-start(bf16[32,2560]{1,0:T(8,128)(2,1)S(1)} %dynamic-slice_convert_fusion.9), channel_id=1, source_target_pairs={{0,8},{1,9},{2,10},{3,11},{4,12},{5,13},{6,14},{7,15},{8,0},{9,1},... | collective-permute-start | bytes 491528 | tf_op jit(solution)/shard_map/ppermute | solution.py:36
  58.8 13.6 %collective-permute-start.18 = (bf16[32,2560]{1,0:T(8,128)(2,1)S(1)}, bf16[32,2560]{1,0:T(8,128)(2,1)S(1)}, u32[]{:S(2)}, u32[]{:S(2)}) collective-permute-start(bf16[32,2560]{1,0:T(8,128)(2,1)S(1)} %dynamic-slice_convert_fusion.10), channel_id=1, source_target_pairs={{0,4},{1,5},{2,6},{3,7},{4,0},{5,1},{6,2},{7,3},{8,12},{9,13},{10,... | collective-permute-start | bytes 491528 | tf_op jit(solution)/shard_map/ppermute | solution.py:36
  61.4 33.6 %collective-permute-start.9 = (bf16[256,1024]{1,0:T(8,128)(2,1)S(1)}, bf16[256,1024]{1,0:T(8,128)(2,1)S(1)}, u32[]{:S(2)}, u32[]{:S(2)}) collective-permute-start(bf16[256,1024]{1,0:T(8,128)(2,1)S(1)} %dynamic-slice_convert_fusion.3), channel_id=1, source_target_pairs={{0,2},{1,3},{2,0},{3,1},{4,6},{5,7},{6,4},{7,5},{8,10},{9,11},{10,... | collective-permute-start | bytes 1572872 | tf_op jit(solution)/shard_map/ppermute | solution.py:36
  72.5 13.8 %collective-permute-start.19 = (bf16[16,2560]{1,0:T(8,128)(2,1)S(1)}, bf16[16,2560]{1,0:T(8,128)(2,1)S(1)}, u32[]{:S(2)}, u32[]{:S(2)}) collective-permute-start(bf16[16,2560]{1,0:T(8,128)(2,1)S(1)} %dynamic-slice_convert_fusion.14), channel_id=1, source_target_pairs={{0,8},{1,9},{2,10},{3,11},{4,12},{5,13},{6,14},{7,15},{8,0},{9,1},... | collective-permute-start | bytes 245768 | tf_op jit(solution)/shard_map/ppermute | solution.py:36
  72.7 24.1 %collective-permute-start.2 = (bf16[128,768]{1,0:T(8,128)(2,1)S(1)}, bf16[128,768]{1,0:T(8,128)(2,1)S(1)}, u32[]{:S(2)}, u32[]{:S(2)}) collective-permute-start(bf16[128,768]{1,0:T(8,128)(2,1)S(1)} %dynamic-slice_convert_fusion.8), channel_id=1, source_target_pairs={{0,8},{1,9},{2,10},{3,11},{4,12},{5,13},{6,14},{7,15},{8,0},{9,1},... | collective-permute-start | bytes 589832 | tf_op jit(solution)/shard_map/ppermute | solution.py:36
  75.3 11.2 %collective-permute-start.28 = (bf16[16,2560]{1,0:T(8,128)(2,1)S(1)}, bf16[16,2560]{1,0:T(8,128)(2,1)S(1)}, u32[]{:S(2)}, u32[]{:S(2)}) collective-permute-start(bf16[16,2560]{1,0:T(8,128)(2,1)S(1)} %add_convert_fusion.2), channel_id=1, source_target_pairs={{0,2},{1,3},{2,0},{3,1},{4,6},{5,7},{6,4},{7,5},{8,10},{9,11},{10,... | collective-permute-start | bytes 245768 | tf_op jit(solution)/shard_map/ppermute | solution.py:36
  86.5 30.7 %collective-permute-start.29 = (bf16[32,2560]{1,0:T(8,128)(2,1)S(1)}, bf16[32,2560]{1,0:T(8,128)(2,1)S(1)}, u32[]{:S(2)}, u32[]{:S(2)}) collective-permute-start(bf16[32,2560]{1,0:T(8,128)(2,1)S(1)} %maximum_select_fusion.15), channel_id=1, source_target_pairs={{0,8},{1,9},{2,10},{3,11},{4,12},{5,13},{6,14},{7,15},{8,0},{9,1},... | collective-permute-start | bytes 491528 | tf_op jit(solution)/shard_map/ppermute | solution.py:36
  95.0 27.9 %collective-permute-start.21 = (bf16[32,2560]{1,0:T(8,128)(2,1)S(1)}, bf16[32,2560]{1,0:T(8,128)(2,1)S(1)}, u32[]{:S(2)}, u32[]{:S(2)}) collective-permute-start(bf16[32,2560]{1,0:T(8,128)(2,1)S(1)} %maximum_select_fusion.14), channel_id=1, source_target_pairs={{0,4},{1,5},{2,6},{3,7},{4,0},{5,1},{6,2},{7,3},{8,12},{9,13},{10,... | collective-permute-start | bytes 491528 | tf_op jit(solution)/shard_map/ppermute | solution.py:36
  95.3 12.1 %collective-permute-start.10 = (bf16[128,1024]{1,0:T(8,128)(2,1)S(1)}, bf16[128,1024]{1,0:T(8,128)(2,1)S(1)}, u32[]{:S(2)}, u32[]{:S(2)}) collective-permute-start(bf16[128,1024]{1,0:T(8,128)(2,1)S(1)} %dynamic-slice_convert_fusion.7), channel_id=1, source_target_pairs={{0,4},{1,5},{2,6},{3,7},{4,0},{5,1},{6,2},{7,3},{8,12},{9,13},{10,... | collective-permute-start | bytes 786440 | tf_op jit(solution)/shard_map/ppermute | solution.py:36
  96.9 10.7 %collective-permute-start.3 = (bf16[64,768]{1,0:T(8,128)(2,1)S(1)}, bf16[64,768]{1,0:T(8,128)(2,1)S(1)}, u32[]{:S(2)}, u32[]{:S(2)}) collective-permute-start(bf16[64,768]{1,0:T(8,128)(2,1)S(1)} %dynamic-slice_convert_fusion.12), channel_id=1, source_target_pairs={{0,2},{1,3},{2,0},{3,1},{4,6},{5,7},{6,4},{7,5},{8,10},{9,11},{10,... | collective-permute-start | bytes 294920 | tf_op jit(solution)/shard_map/ppermute | solution.py:36
  107.5 9.6 %collective-permute-start.11 = (bf16[64,1024]{1,0:T(8,128)(2,1)S(1)}, bf16[64,1024]{1,0:T(8,128)(2,1)S(1)}, u32[]{:S(2)}, u32[]{:S(2)}) collective-permute-start(bf16[64,1024]{1,0:T(8,128)(2,1)S(1)} %dynamic-slice_convert_fusion.11), channel_id=1, source_target_pairs={{0,8},{1,9},{2,10},{3,11},{4,12},{5,13},{6,14},{7,15},{8,0},{9,1},... | collective-permute-start | bytes 393224 | tf_op jit(solution)/shard_map/ppermute | solution.py:36
  107.6 9.7 %collective-permute-start.4 = (bf16[64,768]{1,0:T(8,128)(2,1)S(1)}, bf16[64,768]{1,0:T(8,128)(2,1)S(1)}, u32[]{:S(2)}, u32[]{:S(2)}) collective-permute-start(bf16[64,768]{1,0:T(8,128)(2,1)S(1)} %add_convert_fusion.1), channel_id=1, source_target_pairs={{0,2},{1,3},{2,0},{3,1},{4,6},{5,7},{6,4},{7,5},{8,10},{9,11},{10,... | collective-permute-start | bytes 294920 | tf_op jit(solution)/shard_map/ppermute | solution.py:36
  117.3 22.0 %collective-permute-start.30 = (bf16[64,2560]{1,0:T(8,128)(2,1)S(1)}, bf16[64,2560]{1,0:T(8,128)(2,1)S(1)}, u32[]{:S(2)}, u32[]{:S(2)}) collective-permute-start(bf16[64,2560]{1,0:T(8,128)(2,1)S(1)} %maximum_select_fusion.11), channel_id=1, source_target_pairs={{0,4},{1,5},{2,6},{3,7},{4,0},{5,1},{6,2},{7,3},{8,12},{9,13},{10,... | collective-permute-start | bytes 983048 | tf_op jit(solution)/shard_map/ppermute | solution.py:36
  117.4 13.8 %collective-permute-start.5 = (bf16[128,768]{1,0:T(8,128)(2,1)S(1)}, bf16[128,768]{1,0:T(8,128)(2,1)S(1)}, u32[]{:S(2)}, u32[]{:S(2)}) collective-permute-start(bf16[128,768]{1,0:T(8,128)(2,1)S(1)} %maximum_select_fusion.13), channel_id=1, source_target_pairs={{0,8},{1,9},{2,10},{3,11},{4,12},{5,13},{6,14},{7,15},{8,0},{9,1},... | collective-permute-start | bytes 589832 | tf_op jit(solution)/shard_map/ppermute | solution.py:36
  122.8 16.1 %collective-permute-start.13 = (bf16[128,1024]{1,0:T(8,128)(2,1)S(1)}, bf16[128,1024]{1,0:T(8,128)(2,1)S(1)}, u32[]{:S(2)}, u32[]{:S(2)}) collective-permute-start(bf16[128,1024]{1,0:T(8,128)(2,1)S(1)} %maximum_select_fusion.12), channel_id=1, source_target_pairs={{0,4},{1,5},{2,6},{3,7},{4,0},{5,1},{6,2},{7,3},{8,12},{9,13},{10,... | collective-permute-start | bytes 786440 | tf_op jit(solution)/shard_map/ppermute | solution.py:36
  122.9 18.9 %collective-permute-start.22 = (bf16[64,2560]{1,0:T(8,128)(2,1)S(1)}, bf16[64,2560]{1,0:T(8,128)(2,1)S(1)}, u32[]{:S(2)}, u32[]{:S(2)}) collective-permute-start(bf16[64,2560]{1,0:T(8,128)(2,1)S(1)} %maximum_select_fusion.10), channel_id=1, source_target_pairs={{0,2},{1,3},{2,0},{3,1},{4,6},{5,7},{6,4},{7,5},{8,10},{9,11},{10,... | collective-permute-start | bytes 983048 | tf_op jit(solution)/shard_map/ppermute | solution.py:36
  131.3 22.7 %collective-permute-start.6 = (bf16[256,768]{1,0:T(8,128)(2,1)S(1)}, bf16[256,768]{1,0:T(8,128)(2,1)S(1)}, u32[]{:S(2)}, u32[]{:S(2)}) collective-permute-start(bf16[256,768]{1,0:T(8,128)(2,1)S(1)} %maximum_select_fusion.9), channel_id=1, source_target_pairs={{0,4},{1,5},{2,6},{3,7},{4,0},{5,1},{6,2},{7,3},{8,12},{9,13},{10,... | collective-permute-start | bytes 1179656 | tf_op jit(solution)/shard_map/ppermute | solution.py:36
  139.0 11.4 %collective-permute-start.14 = (bf16[256,1024]{1,0:T(8,128)(2,1)S(1)}, bf16[256,1024]{1,0:T(8,128)(2,1)S(1)}, u32[]{:S(2)}, u32[]{:S(2)}) collective-permute-start(bf16[256,1024]{1,0:T(8,128)(2,1)S(1)} %maximum_select_fusion.8), channel_id=1, source_target_pairs={{0,2},{1,3},{2,0},{3,1},{4,6},{5,7},{6,4},{7,5},{8,10},{9,11},{10,... | collective-permute-start | bytes 1572872 | tf_op jit(solution)/shard_map/ppermute | solution.py:36
  139.4 15.0 %collective-permute-start.31 = (bf16[128,2560]{1,0:T(8,128)(2,1)S(1)}, bf16[128,2560]{1,0:T(8,128)(2,1)}, u32[]{:S(2)}, u32[]{:S(2)}) collective-permute-start(bf16[128,2560]{1,0:T(8,128)(2,1)S(1)} %maximum_select_fusion.7), channel_id=1, source_target_pairs={{0,1},{1,0},{2,3},{3,2},{4,5},{5,4},{6,7},{7,6},{8,9},{9,8},{10,11... | collective-permute-start | bytes 1966088 | tf_op jit(solution)/shard_map/ppermute | solution.py:36
  141.9 14.1 %collective-permute-start.23 = (bf16[128,2560]{1,0:T(8,128)(2,1)S(1)}, bf16[128,2560]{1,0:T(8,128)(2,1)}, u32[]{:S(2)}, u32[]{:S(2)}) collective-permute-start(bf16[128,2560]{1,0:T(8,128)(2,1)S(1)} %maximum_select_fusion.6), channel_id=1, source_target_pairs={{0,1},{1,0},{2,3},{3,2},{4,5},{5,4},{6,7},{7,6},{8,9},{9,8},{10,11... | collective-permute-start | bytes 1966088 | tf_op jit(solution)/shard_map/ppermute | solution.py:36
  (22 other events, 231.7 us)

commit v2 on v1

--- a/solution.py
+++ b/solution.py
@@ -25,11 +25,16 @@
     )
 
 
-def upper_blocks(array):
-    order = array.shape[1]
-    return jnp.concatenate(
-        [contract(array[:, k : k + BLOCK], array[:, k:]) for k in range(0, order, BLOCK)], axis=1
-    )
+def strips(first, second):
+    return [
+        contract(first[:, k : k + BLOCK], second) for k in range(0, first.shape[1], BLOCK)
+    ]
+
+
+def upper_strips(array):
+    return [
+        contract(array[:, k : k + BLOCK], array[:, k:]) for k in range(0, array.shape[1], BLOCK)
+    ]
 
 
 def exchange(value, bit, count):
@@ -67,17 +72,29 @@
     for block in blocks:
         joined = jnp.concatenate([block, eye], axis=1)
         tables.append([joined[8 * c : 8 * c + 8] for c in range(rows)])
-    for j in range(size):
+    wide = (8, 2 * size)
+    for j in range(0, size, 2):
         c0, r0 = j // 8, j % 8
         for t in tables:
-            row = jnp.broadcast_to(t[c0][r0 : r0 + 1, :], (8, 2 * size))
-            inv = 1.0 / jnp.broadcast_to(row[:, j : j + 1], (8, 2 * size))
-            scaled = row * inv
-            for c in range(c0, rows):
-                col = jnp.broadcast_to(t[c][:, j : j + 1], (8, 2 * size))
-                if c == c0:
-                    col = jnp.where(sub > r0, col, 0.0)
-                t[c] = t[c] - col * scaled
+            head = t[c0]
+            row0 = jnp.broadcast_to(head[r0 : r0 + 1, :], wide)
+            row1 = jnp.broadcast_to(head[r0 + 1 : r0 + 2, :], wide)
+            a = jnp.broadcast_to(row0[:, j : j + 1], wide)
+            b = jnp.broadcast_to(row1[:, j : j + 1], wide)
+            c = jnp.broadcast_to(row1[:, j + 1 : j + 2], wide)
+            inv = 1.0 / a
+            ratio = b * inv
+            inv1 = 1.0 / (c - ratio * b)
+            lifted = row1 - ratio * row0
+            scaled0 = row0 * inv
+            scaled1 = lifted * inv1
+            for k in range(c0, rows):
+                col0 = jnp.broadcast_to(t[k][:, j : j + 1], wide)
+                col1 = jnp.broadcast_to(t[k][:, j + 1 : j + 2], wide) - ratio * col0
+                if k == c0:
+                    col0 = jnp.where(sub > r0, col0, 0.0)
+                    col1 = jnp.where(sub > r0 + 1, col1, 0.0)
+                t[k] = t[k] - col0 * scaled0 - col1 * scaled1
     out = []
     for t in tables:
         joined = jnp.concatenate(t, axis=0)
@@ -94,15 +111,16 @@
 
 
 def tail_kernel(
-    where_ref, pairing_ref, first_ref, middle_ref, upper_ref, lower_ref,
+    where_ref, pairing_ref, near_ref, far_ref,
     out_up, out_low, moved, loose, gram_ref, table, *, half_rows, units
 ):
-    order, rank2 = first_ref.shape
-    rank = rank2 // 2
+    order, rank = moved.shape
+    sides = order // BLOCK
     unit = order // units
     share = out_up.shape[0]
 
-    loose[...] = first_ref[:, :rank].astype(F32)
+    for k in range(sides):
+        loose[k * BLOCK : (k + 1) * BLOCK, :] = far_ref[:, k * rank : (k + 1) * rank].astype(F32)
 
     @pl.loop(0, units)
     def _(i):
@@ -110,9 +128,23 @@
             pl.ds(pl.multiple_of(i * unit, unit), unit), :
         ]
 
-    third_right = jnp.dot(middle_ref[...], moved[...].astype(BF16), preferred_element_type=F32).astype(BF16)
-    loose[...] = lax.dot_general(
-        middle_ref[...], first_ref[:, rank:], (((0,), (0,)), ((), ())), preferred_element_type=F32
+    swapped = moved[...].astype(BF16)
+    third_right = jnp.concatenate(
+        [
+            jnp.dot(
+                near_ref[:, k * order : (k + 1) * order], swapped, preferred_element_type=F32
+            ).astype(BF16)
+            for k in range(sides)
+        ],
+        axis=0,
+    )
+    left = sides * rank
+    loose[...] = sum(
+        contract(
+            near_ref[:, k * order : (k + 1) * order],
+            far_ref[:, left + k * rank : left + (k + 1) * rank],
+        )
+        for k in range(sides)
     )
 
     @pl.loop(0, units)
@@ -122,8 +154,8 @@
         ]
 
     thirds = (third_right, moved[...].astype(BF16))
-    for s, (third, square_ref) in enumerate(zip(thirds, (upper_ref, lower_ref))):
-        base = 0
+    for s, (third, square_ref) in enumerate(zip(thirds, (near_ref, far_ref))):
+        base = (sides * order, 2 * left)[s]
         parts = [None] * (order // BLOCK)
         for k in range(order // BLOCK):
             width = order - k * BLOCK
@@ -171,16 +203,14 @@
         )
 
 
-def tail(me, pairing, first, middle, upper, lower, half_rows, count):
-    order = first.shape[0]
-    rank = first.shape[1] // 2
+def tail(me, pairing, near, far, order, rank, half_rows, count):
     share = jax.ShapeDtypeStruct((order // count, rank), F32)
     smem = pl.BlockSpec(memory_space=pltpu.SMEM)
     vmem = pl.BlockSpec(memory_space=pltpu.VMEM)
     return pl.pallas_call(
         functools.partial(tail_kernel, half_rows=half_rows, units=count),
         out_shape=(share, share),
-        in_specs=[smem, smem, vmem, vmem, vmem, vmem],
+        in_specs=[smem, smem, vmem, vmem],
         out_specs=(vmem, vmem),
         scratch_shapes=[
             pltpu.VMEM((order, rank), F32),
@@ -189,7 +219,7 @@
             pltpu.VMEM((2, order, rank), F32),
         ],
         compiler_params=pltpu.CompilerParams(vmem_limit_bytes=48 * 2**20),
-    )(me[None], pairing, first, middle, upper, lower)
+    )(me[None], pairing, near, far)
 
 
 def per_device(
@@ -198,19 +228,24 @@
     count = lax.axis_size("cols")
     me = lax.axis_index("cols").astype(jnp.int32)
     half_rows = upper_left.shape[0] * count
+    order, rank = upper_left.shape[1], sketch_right.shape[1]
     bits = list(range(count.bit_length() - 1))
     near_first = bits
     far_first = bits[:1] + bits[2:] + bits[1:2]
-    middle = sum_rows(contract(upper_right, lower_right), near_first, me, count)
-    first = sum_rows(
+    near = sum_rows(
+        jnp.concatenate(strips(upper_right, lower_right) + upper_strips(upper_left), axis=1),
+        near_first, me, count,
+    )
+    far = sum_rows(
         jnp.concatenate(
-            [contract(lower_left, sketch_right), contract(upper_left, sketch_left)], axis=1
+            strips(lower_left, sketch_right)
+            + strips(upper_left, sketch_left)
+            + upper_strips(lower_left),
+            axis=1,
         ),
         far_first, me, count,
     )
-    upper = sum_rows(upper_blocks(upper_left), near_first, me, count)
-    lower = sum_rows(upper_blocks(lower_left), far_first, me, count)
-    return tail(me, pairing, first, middle, upper, lower, half_rows, count)
+    return tail(me, pairing, near, far, order, rank, half_rows, count)
 
 
 def solution(mesh):

time: 244 us -> 229 us (0.939)
  waiting for transfers between devices: 78.8 us -> 103 us
  Pallas kernels: 78.6 us -> 56.7 us
  starting transfers between devices: 22.6 us -> 10.7 us
  other arithmetic: 19.8 us -> 10.4 us
  matrix products: 33.8 us -> 39 us
    ppermute x32 -> x16, waiting for transfers between devices: 78.8 us -> 103 us  [exchange(): lax.ppermute(value, 'cols', [(i, i ^ 1 << bit) for i in range(count)])]
    pallas_call x1, Pallas kernels: 78.6 us -> 56.7 us  [tail(): pl.pallas_call(functools.partial(tail_kernel, half_rows=half_rows, units=...]
    ppermute x32 -> x16, starting transfers between devices: 22.6 us -> 10.7 us  [exchange(): lax.ppermute(value, 'cols', [(i, i ^ 1 << bit) for i in range(count)])]
    dot_general x11 -> x20, matrix products: 33.8 us -> 39 us  [contract(): lax.dot_general(first, second, (((0,), (0,)), ((), ())), preferred_elemen...]
    select_n x16 -> x8, other arithmetic: 10.5 us -> 6.82 us  [sum_rows(): jnp.where(mine == 0, jnp.concatenate([share, other], axis=0), jnp.concate...]
    add x12 -> x6, other arithmetic: 6.51 us -> 3.5 us  [sum_rows(): partial = kept + exchange(sent, bit, count).astype(F32)]
  transfers between devices with their start and end apart: 32 -> 16, of which waited for: 13 -> 12; matrix products, arithmetic and copies ran while one was open for 17% -> 10% of each run, Pallas kernels for 0% -> 0%
where the time goes in v2:
time: 229 us
  waiting for transfers between devices  103 us (45%)
  Pallas kernels  56.7 us (25%)
  matrix products  39 us (17%)
  starting transfers between devices  10.7 us (5%)
  other arithmetic  10.4 us (5%)
  local copies, waits for them, and re-layouts  8.73 us (4%)
    ppermute x16, waiting for transfers between devices, exchange(): lax.ppermute(value, 'cols', [(i, i ^ 1 << bit) for i in range(count)])  103 us
    pallas_call x1, Pallas kernels, tail(): pl.pallas_call(functools.partial(tail_kernel, half_rows=half_rows, units=...  56.7 us
    dot_general x20, matrix products, contract(): lax.dot_general(first, second, (((0,), (0,)), ((), ())), preferred_elemen...  39 us
    ppermute x16, starting transfers between devices, exchange(): lax.ppermute(value, 'cols', [(i, i ^ 1 << bit) for i in range(count)])  10.7 us
    select_n x8, other arithmetic, sum_rows(): jnp.where(mine == 0, jnp.concatenate([share, other], axis=0), jnp.concate...  6.82 us
    unnamed x28, local copies, waits for them, and re-layouts  5.01 us
  transfers between devices with their start and end apart: 16, of which 12 were waited for; matrix products, arithmetic and copies ran while one was open for 10% of the time, Pallas kernels for 0%

profile of v2, /device:TPU:29, one launch (start us, length us, event | category | flops | bytes accessed | tf_op | source)
XLA Modules:
  0.0 229.1 jit_solution(8811825090349204474)
XLA Ops:
  2.1 3.1 %convolution_dynamic-update-slice_fusion.13 = f32[256,5632]{1,0:T(8,128)} fusion(bf16[2400,384]{1,0:T(8,128)(2,1)S(1)} %copy-done, bf16[2400,1024]{1,0:T(8,128)(2,1)} %param.9), kind=kOutput, calls=%fused_computation.37 | convolution fusion | flops 471859200 | bytes 3465216 | tf_op jit(solution)/shard_map/dot_general | solution.py:17
  5.2 2.9 %convolution_dynamic-update-slice_fusion.12 = f32[256,5632]{1,0:T(8,128)} fusion(f32[256,5632]{1,0:T(8,128)} %convolution_dynamic-update-slice_fusion.13, bf16[2400,384]{1,0:T(8,128)(2,1)S(1)} %copy-done, bf16[2400,1024]{1,0:T(8,128)(2,1)} %param.9), kind=kOutput, calls=%fused_computation.36 | convolution fusion | flops 471859200 | bytes 3465216 | tf_op jit(solution)/shard_map/dot_general | solution.py:17
  18.3 2.6 %convolution_dynamic-update-slice_fusion = f32[256,5632]{1,0:T(8,128)} fusion(f32[256,5632]{1,0:T(8,128)} %convolution_dynamic-update-slice_fusion.6, bf16[2400,1024]{1,0:T(8,128)(2,1)S(1)} %copy-done.4), kind=kOutput, calls=%fused_computation.17 | convolution fusion | flops 1258291200 | bytes 7192576 | tf_op jit(solution)/shard_map/dot_general | solution.py:17
  21.0 2.1 fusion.11
  26.1 3.2 %dynamic-slice_convert_fusion.1 = bf16[128,5632]{1,0:T(8,128)(2,1)} fusion(f32[256,5632]{1,0:T(8,128)} %convolution_dynamic-update-slice_fusion.14, s32[]{:T(128)S(6)} %select_n.113), kind=kLoop, calls=%fused_computation.9 | loop fusion | bytes 2883588 | tf_op jit(solution)/shard_map/convert_element_type | solution.py:49
  30.0 4.7 %convolution_dynamic-update-slice_fusion.5 = f32[256,6656]{1,0:T(8,128)S(1)} fusion(bf16[2400,1024]{1,0:T(8,128)(2,1)} %param.10, bf16[2400,1024]{1,0:T(8,128)(2,1)} %param.8), kind=kOutput, calls=%fused_computation.22 | convolution fusion | flops 1258291200 | bytes 7192576 | tf_op jit(solution)/shard_map/dot_general | solution.py:17
  34.7 3.0 %convolution_dynamic-update-slice_fusion.4 = f32[256,6656]{1,0:T(8,128)S(1)} fusion(f32[256,6656]{1,0:T(8,128)S(1)} %convolution_dynamic-update-slice_fusion.5, bf16[2400,1024]{1,0:T(8,128)(2,1)S(1)} %bitcast.18, bf16[2400,1024]{1,0:T(8,128)(2,1)} %param.8), kind=kOutput, calls=%fused_computation.21 | convolution fusion | flops 1258291200 | bytes 7192576 | tf_op jit(solution)/shard_map/dot_general | solution.py:17
  45.2 2.8 %copy-done.6 = f32[256,6656]{1,0:T(8,128)} copy-done((f32[256,6656]{1,0:T(8,128)}, f32[256,6656]{1,0:T(8,128)S(1)}, u32[]{:S(2)}) %copy-start.6) | copy-done | bytes 6815768
  48.3 2.7 %convert_add_fusion.1 = f32[128,5632]{1,0:T(8,128)S(1)} fusion(bf16[128,5632]{1,0:T(8,128)(2,1)} %collective-permute-done.8, f32[256,5632]{1,0:T(8,128)} %convolution_dynamic-update-slice_fusion.14, s32[]{:T(128)S(6)} %select_n.112), kind=kLoop, calls=%fused_computation.8 | loop fusion | flops 1441792 | bytes 7208964 | tf_op jit(solution)/shard_map/add | solution.py:50
  52.9 15.5 %collective-permute-done.9 = bf16[64,5632]{1,0:T(8,128)(2,1)S(1)} collective-permute-done((bf16[64,5632]{1,0:T(8,128)(2,1)S(1)}, bf16[64,5632]{1,0:T(8,128)(2,1)S(1)}, u32[]{:S(2)}, u32[]{:S(2)}) %collective-permute-start.9) | collective-permute-done | bytes 720928 | tf_op jit(solution)/shard_map/ppermute | solution.py:41
  69.0 18.4 %collective-permute-done.10 = bf16[32,5632]{1,0:T(8,128)(2,1)S(1)} collective-permute-done((bf16[32,5632]{1,0:T(8,128)(2,1)S(1)}, bf16[32,5632]{1,0:T(8,128)(2,1)S(1)}, u32[]{:S(2)}, u32[]{:S(2)}) %collective-permute-start.10) | collective-permute-done | bytes 360480 | tf_op jit(solution)/shard_map/ppermute | solution.py:41
  88.9 7.9 %collective-permute-done.2 = bf16[32,6656]{1,0:T(8,128)(2,1)S(1)} collective-permute-done((bf16[32,6656]{1,0:T(8,128)(2,1)S(1)}, bf16[32,6656]{1,0:T(8,128)(2,1)S(1)}, u32[]{:S(2)}, u32[]{:S(2)}) %collective-permute-start.2) | collective-permute-done | bytes 426016 | tf_op jit(solution)/shard_map/ppermute | solution.py:41
  97.0 2.4 %collective-permute-start.3 = (bf16[16,6656]{1,0:T(8,128)(2,1)S(1)}, bf16[16,6656]{1,0:T(8,128)(2,1)S(1)}, u32[]{:S(2)}, u32[]{:S(2)}) collective-permute-start(bf16[16,6656]{1,0:T(8,128)(2,1)S(1)} %dynamic-slice_convert_fusion.6), channel_id=1, source_target_pairs={{0,8},{1,9},{2,10},{3,11},{4,12},{5,13},{6,14},{7,15},{8,0},{9,1},... | collective-permute-start | bytes 638984 | tf_op jit(solution)/shard_map/ppermute | solution.py:41
  99.7 8.5 %collective-permute-done.3 = bf16[16,6656]{1,0:T(8,128)(2,1)S(1)} collective-permute-done((bf16[16,6656]{1,0:T(8,128)(2,1)S(1)}, bf16[16,6656]{1,0:T(8,128)(2,1)S(1)}, u32[]{:S(2)}, u32[]{:S(2)}) %collective-permute-start.3) | collective-permute-done | bytes 213024 | tf_op jit(solution)/shard_map/ppermute | solution.py:41
  108.3 2.4 %collective-permute-start.13 = (bf16[32,5632]{1,0:T(8,128)(2,1)S(1)}, bf16[32,5632]{1,0:T(8,128)(2,1)S(1)}, u32[]{:S(2)}, u32[]{:S(2)}) collective-permute-start(bf16[32,5632]{1,0:T(8,128)(2,1)S(1)} %maximum_select_fusion.7), channel_id=1, source_target_pairs={{0,8},{1,9},{2,10},{3,11},{4,12},{5,13},{6,14},{7,15},{8,0},{9,1},... | collective-permute-start | bytes 1081352 | tf_op jit(solution)/shard_map/ppermute | solution.py:41
  110.7 13.3 %collective-permute-done.4 = bf16[16,6656]{1,0:T(8,128)(2,1)S(1)} collective-permute-done((bf16[16,6656]{1,0:T(8,128)(2,1)S(1)}, bf16[16,6656]{1,0:T(8,128)(2,1)S(1)}, u32[]{:S(2)}, u32[]{:S(2)}) %collective-permute-start.4) | collective-permute-done | bytes 213024 | tf_op jit(solution)/shard_map/ppermute | solution.py:41
  124.2 5.0 %collective-permute-done.13 = bf16[32,5632]{1,0:T(8,128)(2,1)S(1)} collective-permute-done((bf16[32,5632]{1,0:T(8,128)(2,1)S(1)}, bf16[32,5632]{1,0:T(8,128)(2,1)S(1)}, u32[]{:S(2)}, u32[]{:S(2)}) %collective-permute-start.13) | collective-permute-done | bytes 360480 | tf_op jit(solution)/shard_map/ppermute | solution.py:41
  129.3 14.0 %collective-permute-done.5 = bf16[32,6656]{1,0:T(8,128)(2,1)S(1)} collective-permute-done((bf16[32,6656]{1,0:T(8,128)(2,1)S(1)}, bf16[32,6656]{1,0:T(8,128)(2,1)S(1)}, u32[]{:S(2)}, u32[]{:S(2)}) %collective-permute-start.5) | collective-permute-done | bytes 426016 | tf_op jit(solution)/shard_map/ppermute | solution.py:41
  143.8 15.0 %collective-permute-done.14 = bf16[64,5632]{1,0:T(8,128)(2,1)S(1)} collective-permute-done((bf16[64,5632]{1,0:T(8,128)(2,1)S(1)}, bf16[64,5632]{1,0:T(8,128)(2,1)S(1)}, u32[]{:S(2)}, u32[]{:S(2)}) %collective-permute-start.14) | collective-permute-done | bytes 720928 | tf_op jit(solution)/shard_map/ppermute | solution.py:41
  159.6 2.9 %collective-permute-done.6 = bf16[64,6656]{1,0:T(8,128)(2,1)S(1)} collective-permute-done((bf16[64,6656]{1,0:T(8,128)(2,1)S(1)}, bf16[64,6656]{1,0:T(8,128)(2,1)S(1)}, u32[]{:S(2)}, u32[]{:S(2)}) %collective-permute-start.6) | collective-permute-done | bytes 852000 | tf_op jit(solution)/shard_map/ppermute | solution.py:41
  162.8 2.4 %collective-permute-start.7 = (bf16[128,6656]{1,0:T(8,128)(2,1)S(1)}, bf16[128,6656]{1,0:T(8,128)(2,1)}, u32[]{:S(2)}, u32[]{:S(2)}) collective-permute-start(bf16[128,6656]{1,0:T(8,128)(2,1)S(1)} %maximum_select_fusion.2), channel_id=1, source_target_pairs={{0,1},{1,0},{2,3},{3,2},{4,5},{5,4},{6,7},{7,6},{8,9},{9,8},{10,11... | collective-permute-start | bytes 5111816 | tf_op jit(solution)/shard_map/ppermute | solution.py:41
  165.3 2.2 maximum_select_fusion.1.far_ref
  168.6 3.7 %maximum_select_fusion.near_ref = bf16[256,6656]{1,0:T(8,128)(2,1)} fusion(bf16[128,6656]{1,0:T(8,128)(2,1)} %collective-permute-done.7, bf16[128,6656]{1,0:T(8,128)(2,1)S(1)} %maximum_select_fusion.2, pred[]{:T(512)S(6)} %eq.16), kind=kLoop, calls=%fused_computation.4 | loop fusion | flops 15335424 | bytes 6815745 | tf_op jit(solution)/shard_map/jit(_where)/select_n | solution.py:55
  172.4 56.7 %shard_map.86 = (f32[64,384]{1,0:T(8,128)}, f32[64,384]{1,0:T(8,128)}) custom-call(s32[1]{0:T(128)} %bitcast.where_ref, s32[16]{0:T(128)S(1)} %copy-done.2, bf16[256,6656]{1,0:T(8,128)(2,1)} %maximum_select_fusion.near_ref, bf16[256,5632]{1,0:T(8,128)(2,1)S(1)} %maximum_select_fusion.1.far_ref), custom_call_target="tpu_custom_call" | custom-call | tf_op jit(solution)/shard_map/pallas_call | solution.py:210
  (84 shorter events, 30.5 us)
Async XLA Ops:
  2.1 6.0 %copy-start.4 = (bf16[2400,1024]{1,0:T(8,128)(2,1)S(1)}, bf16[2400,1024]{1,0:T(8,128)(2,1)}, u32[]{:S(2)}) copy-start(bf16[2400,1024]{1,0:T(8,128)(2,1)} %param.9) | copy-start | bytes 14745604
  24.8 12.9 %slice-start.4 = ((s8[4915200]{0:T(1024)(128)(4,1)}), s8[720896]{0:T(1024)(128)(4,1)S(1)}, s32[]{:S(2)}) async-start(s8[4915200]{0:T(1024)(128)(4,1)} %bitcast.19), calls=%async_computation.4 | async-start | bytes 1441792
  26.1 8.6 %slice-start.2 = ((s8[4915200]{0:T(1024)(128)(4,1)}), s8[4194304]{0:T(1024)(128)(4,1)S(1)}, s32[]{:S(2)}) async-start(s8[4915200]{0:T(1024)(128)(4,1)} %bitcast.17), calls=%async_computation.2 | async-start | bytes 8388608
  29.3 5.4 %slice-start.3 = ((s8[4915200]{0:T(1024)(128)(4,1)}), s8[720896]{0:T(1024)(128)(4,1)S(1)}, s32[]{:S(2)}) async-start(s8[4915200]{0:T(1024)(128)(4,1)} %bitcast.17), calls=%async_computation.3 | async-start | bytes 1441792
  29.3 8.4 %slice-start.5 = ((s8[4915200]{0:T(1024)(128)(4,1)}), s8[4194304]{0:T(1024)(128)(4,1)S(1)}, s32[]{:S(2)}) async-start(s8[4915200]{0:T(1024)(128)(4,1)} %bitcast.19), calls=%async_computation.5 | async-start | bytes 8388608
  29.3 19.0 %collective-permute-start.8 = (bf16[128,5632]{1,0:T(8,128)(2,1)}, bf16[128,5632]{1,0:T(8,128)(2,1)}, u32[]{:S(2)}, u32[]{:S(2)}) collective-permute-start(bf16[128,5632]{1,0:T(8,128)(2,1)} %dynamic-slice_convert_fusion.1), channel_id=1, source_target_pairs={{0,1},{1,0},{2,3},{3,2},{4,5},{5,4},{6,7},{7,6},{8,9},{9,8},{10,11... | collective-permute-start | bytes 4325384 | tf_op jit(solution)/shard_map/ppermute | solution.py:41
  48.2 3.7 %collective-permute-start = (bf16[128,6656]{1,0:T(8,128)(2,1)S(1)}, bf16[128,6656]{1,0:T(8,128)(2,1)S(1)}, u32[]{:S(2)}, u32[]{:S(2)}) collective-permute-start(bf16[128,6656]{1,0:T(8,128)(2,1)S(1)} %dynamic-slice_convert_fusion), channel_id=1, source_target_pairs={{0,1},{1,0},{2,3},{3,2},{4,5},{5,4},{6,7},{7,6},{8,9},{9,8},{10,11... | collective-permute-start | bytes 5111816 | tf_op jit(solution)/shard_map/ppermute | solution.py:41
  48.3 4.2 %copy-start.7 = (f32[256,6656]{1,0:T(8,128)S(1)}, f32[256,6656]{1,0:T(8,128)}, u32[]{:S(2)}) copy-start(f32[256,6656]{1,0:T(8,128)} %copy-done.6) | copy-start | bytes 20447236
  51.1 17.3 %collective-permute-start.9 = (bf16[64,5632]{1,0:T(8,128)(2,1)S(1)}, bf16[64,5632]{1,0:T(8,128)(2,1)S(1)}, u32[]{:S(2)}, u32[]{:S(2)}) collective-permute-start(bf16[64,5632]{1,0:T(8,128)(2,1)S(1)} %dynamic-slice_convert_fusion.3), channel_id=1, source_target_pairs={{0,4},{1,5},{2,6},{3,7},{4,0},{5,1},{6,2},{7,3},{8,12},{9,13},{10,... | collective-permute-start | bytes 2162696 | tf_op jit(solution)/shard_map/ppermute | solution.py:41
  68.6 18.8 %collective-permute-start.10 = (bf16[32,5632]{1,0:T(8,128)(2,1)S(1)}, bf16[32,5632]{1,0:T(8,128)(2,1)S(1)}, u32[]{:S(2)}, u32[]{:S(2)}) collective-permute-start(bf16[32,5632]{1,0:T(8,128)(2,1)S(1)} %dynamic-slice_convert_fusion.5), channel_id=1, source_target_pairs={{0,8},{1,9},{2,10},{3,11},{4,12},{5,13},{6,14},{7,15},{8,0},{9,1},... | collective-permute-start | bytes 1081352 | tf_op jit(solution)/shard_map/ppermute | solution.py:41
  68.8 19.0 %collective-permute-start.1 = (bf16[64,6656]{1,0:T(8,128)(2,1)S(1)}, bf16[64,6656]{1,0:T(8,128)(2,1)S(1)}, u32[]{:S(2)}, u32[]{:S(2)}) collective-permute-start(bf16[64,6656]{1,0:T(8,128)(2,1)S(1)} %dynamic-slice_convert_fusion.2), channel_id=1, source_target_pairs={{0,2},{1,3},{2,0},{3,1},{4,6},{5,7},{6,4},{7,5},{8,10},{9,11},{10,... | collective-permute-start | bytes 2555912 | tf_op jit(solution)/shard_map/ppermute | solution.py:41
  88.0 8.9 %collective-permute-start.2 = (bf16[32,6656]{1,0:T(8,128)(2,1)S(1)}, bf16[32,6656]{1,0:T(8,128)(2,1)S(1)}, u32[]{:S(2)}, u32[]{:S(2)}) collective-permute-start(bf16[32,6656]{1,0:T(8,128)(2,1)S(1)} %dynamic-slice_convert_fusion.4), channel_id=1, source_target_pairs={{0,4},{1,5},{2,6},{3,7},{4,0},{5,1},{6,2},{7,3},{8,12},{9,13},{10,... | collective-permute-start | bytes 1277960 | tf_op jit(solution)/shard_map/ppermute | solution.py:41
  88.2 11.2 %collective-permute-start.11 = (bf16[16,5632]{1,0:T(8,128)(2,1)S(1)}, bf16[16,5632]{1,0:T(8,128)(2,1)S(1)}, u32[]{:S(2)}, u32[]{:S(2)}) collective-permute-start(bf16[16,5632]{1,0:T(8,128)(2,1)S(1)} %dynamic-slice_convert_fusion.7), channel_id=1, source_target_pairs={{0,2},{1,3},{2,0},{3,1},{4,6},{5,7},{6,4},{7,5},{8,10},{9,11},{10,... | collective-permute-start | bytes 540680 | tf_op jit(solution)/shard_map/ppermute | solution.py:41
  97.0 11.1 %collective-permute-start.3 = (bf16[16,6656]{1,0:T(8,128)(2,1)S(1)}, bf16[16,6656]{1,0:T(8,128)(2,1)S(1)}, u32[]{:S(2)}, u32[]{:S(2)}) collective-permute-start(bf16[16,6656]{1,0:T(8,128)(2,1)S(1)} %dynamic-slice_convert_fusion.6), channel_id=1, source_target_pairs={{0,8},{1,9},{2,10},{3,11},{4,12},{5,13},{6,14},{7,15},{8,0},{9,1},... | collective-permute-start | bytes 638984 | tf_op jit(solution)/shard_map/ppermute | solution.py:41
  99.4 8.8 %collective-permute-start.12 = (bf16[16,5632]{1,0:T(8,128)(2,1)S(1)}, bf16[16,5632]{1,0:T(8,128)(2,1)S(1)}, u32[]{:S(2)}, u32[]{:S(2)}) collective-permute-start(bf16[16,5632]{1,0:T(8,128)(2,1)S(1)} %add_convert_fusion.1), channel_id=1, source_target_pairs={{0,2},{1,3},{2,0},{3,1},{4,6},{5,7},{6,4},{7,5},{8,10},{9,11},{10,... | collective-permute-start | bytes 540680 | tf_op jit(solution)/shard_map/ppermute | solution.py:41
  108.2 15.9 %collective-permute-start.4 = (bf16[16,6656]{1,0:T(8,128)(2,1)S(1)}, bf16[16,6656]{1,0:T(8,128)(2,1)S(1)}, u32[]{:S(2)}, u32[]{:S(2)}) collective-permute-start(bf16[16,6656]{1,0:T(8,128)(2,1)S(1)} %add_convert_fusion), channel_id=1, source_target_pairs={{0,8},{1,9},{2,10},{3,11},{4,12},{5,13},{6,14},{7,15},{8,0},{9,1},... | collective-permute-start | bytes 638984 | tf_op jit(solution)/shard_map/ppermute | solution.py:41
  108.3 20.8 %collective-permute-start.13 = (bf16[32,5632]{1,0:T(8,128)(2,1)S(1)}, bf16[32,5632]{1,0:T(8,128)(2,1)S(1)}, u32[]{:S(2)}, u32[]{:S(2)}) collective-permute-start(bf16[32,5632]{1,0:T(8,128)(2,1)S(1)} %maximum_select_fusion.7), channel_id=1, source_target_pairs={{0,8},{1,9},{2,10},{3,11},{4,12},{5,13},{6,14},{7,15},{8,0},{9,1},... | collective-permute-start | bytes 1081352 | tf_op jit(solution)/shard_map/ppermute | solution.py:41
  124.1 19.3 %collective-permute-start.5 = (bf16[32,6656]{1,0:T(8,128)(2,1)S(1)}, bf16[32,6656]{1,0:T(8,128)(2,1)S(1)}, u32[]{:S(2)}, u32[]{:S(2)}) collective-permute-start(bf16[32,6656]{1,0:T(8,128)(2,1)S(1)} %maximum_select_fusion.6), channel_id=1, source_target_pairs={{0,4},{1,5},{2,6},{3,7},{4,0},{5,1},{6,2},{7,3},{8,12},{9,13},{10,... | collective-permute-start | bytes 1277960 | tf_op jit(solution)/shard_map/ppermute | solution.py:41
  129.3 29.5 %collective-permute-start.14 = (bf16[64,5632]{1,0:T(8,128)(2,1)S(1)}, bf16[64,5632]{1,0:T(8,128)(2,1)S(1)}, u32[]{:S(2)}, u32[]{:S(2)}) collective-permute-start(bf16[64,5632]{1,0:T(8,128)(2,1)S(1)} %maximum_select_fusion.5), channel_id=1, source_target_pairs={{0,4},{1,5},{2,6},{3,7},{4,0},{5,1},{6,2},{7,3},{8,12},{9,13},{10,... | collective-permute-start | bytes 2162696 | tf_op jit(solution)/shard_map/ppermute | solution.py:41
  143.5 19.0 %collective-permute-start.6 = (bf16[64,6656]{1,0:T(8,128)(2,1)S(1)}, bf16[64,6656]{1,0:T(8,128)(2,1)S(1)}, u32[]{:S(2)}, u32[]{:S(2)}) collective-permute-start(bf16[64,6656]{1,0:T(8,128)(2,1)S(1)} %maximum_select_fusion.4), channel_id=1, source_target_pairs={{0,2},{1,3},{2,0},{3,1},{4,6},{5,7},{6,4},{7,5},{8,10},{9,11},{10,... | collective-permute-start | bytes 2555912 | tf_op jit(solution)/shard_map/ppermute | solution.py:41
  159.1 6.2 %collective-permute-start.15 = (bf16[128,5632]{1,0:T(8,128)(2,1)S(1)}, bf16[128,5632]{1,0:T(8,128)(2,1)}, u32[]{:S(2)}, u32[]{:S(2)}) collective-permute-start(bf16[128,5632]{1,0:T(8,128)(2,1)S(1)} %maximum_select_fusion.3), channel_id=1, source_target_pairs={{0,1},{1,0},{2,3},{3,2},{4,5},{5,4},{6,7},{7,6},{8,9},{9,8},{10,11... | collective-permute-start | bytes 4325384 | tf_op jit(solution)/shard_map/ppermute | solution.py:41
  162.8 5.8 %collective-permute-start.7 = (bf16[128,6656]{1,0:T(8,128)(2,1)S(1)}, bf16[128,6656]{1,0:T(8,128)(2,1)}, u32[]{:S(2)}, u32[]{:S(2)}) collective-permute-start(bf16[128,6656]{1,0:T(8,128)(2,1)S(1)} %maximum_select_fusion.2), channel_id=1, source_target_pairs={{0,1},{1,0},{2,3},{3,2},{4,5},{5,4},{6,7},{7,6},{8,9},{9,8},{10,11... | collective-permute-start | bytes 5111816 | tf_op jit(solution)/shard_map/ppermute | solution.py:41
  167.5 4.9 %copy-start.2 = (s32[16]{0:T(128)S(1)}, s32[16]{0:T(128)}, u32[]{:S(2)}) copy-start(s32[16]{0:T(128)} %pairing_ref.1) | copy-start | bytes 196
  168.6 60.5 %copy-start.1 = (bf16[2400,384]{1,0:T(8,128)(2,1)S(1)}, bf16[2400,384]{1,0:T(8,128)(2,1)}, u32[]{:S(2)}) copy-start(bf16[2400,384]{1,0:T(8,128)(2,1)} %param.11) | copy-start | bytes 5529604
  (6 other events, 15.8 us)

commit v3 on v2

--- a/solution.py
+++ b/solution.py
@@ -41,23 +41,36 @@
     return lax.ppermute(value, "cols", [(i, i ^ (1 << bit)) for i in range(count)])
 
 
-def sum_rows(partial, bits, me, count):
-    for bit in bits:
-        half = partial.shape[0] // 2
-        mine = (me >> bit) & 1
-        kept = lax.dynamic_slice_in_dim(partial, mine * half, half, 0)
-        sent = lax.dynamic_slice_in_dim(partial, (1 - mine) * half, half, 0).astype(BF16)
-        partial = kept + exchange(sent, bit, count).astype(F32)
-    share = partial.astype(BF16)
-    for bit in reversed(bits):
-        mine = (me >> bit) & 1
-        other = exchange(share, bit, count)
-        share = jnp.where(
-            mine == 0,
-            jnp.concatenate([share, other], axis=0),
-            jnp.concatenate([other, share], axis=0),
-        )
-    return share
+def exchange_all(values, bits, count, together):
+    if together:
+        values = lax.optimization_barrier(tuple(values))
+    return tuple(exchange(value, bit, count) for value, bit in zip(values, bits))
+
+
+def sum_rows(partials, orders, me, count):
+    for stage, bits in enumerate(zip(*orders)):
+        kept, sent = [], []
+        for partial, bit in zip(partials, bits):
+            half = partial.shape[0] // 2
+            mine = (me >> bit) & 1
+            kept.append(lax.dynamic_slice_in_dim(partial, mine * half, half, 0))
+            sent.append(
+                lax.dynamic_slice_in_dim(partial, (1 - mine) * half, half, 0).astype(BF16)
+            )
+        others = exchange_all(sent, bits, count, stage == 1)
+        partials = [k + other.astype(F32) for k, other in zip(kept, others)]
+    shares = [partial.astype(BF16) for partial in partials]
+    for bits in reversed(list(zip(*orders))):
+        others = exchange_all(shares, bits, count, False)
+        shares = [
+            jnp.where(
+                (me >> bit) & 1 == 0,
+                jnp.concatenate([share, other], axis=0),
+                jnp.concatenate([other, share], axis=0),
+            )
+            for share, other, bit in zip(shares, others, bits)
+        ]
+    return shares
 
 
 def inverse_factors(blocks):
@@ -176,7 +189,10 @@
         for k in range(order // BLOCK):
             table[s, k * BLOCK : (k + 1) * BLOCK, :] = parts[k]
         product = table[s]
-        gram = sum(contract(third, piece) for piece in split3(product)) * (1.0 / half_rows)
+        pieces = contract(third, jnp.concatenate(split3(product), axis=1))
+        gram = (
+            pieces[:, :rank] + pieces[:, rank : 2 * rank] + pieces[:, 2 * rank :]
+        ) * (1.0 / half_rows)
         gram_ref[s, :, :rank] = gram
         gram_ref[s, :, rank:] = (
             lax.broadcasted_iota(jnp.int32, (rank, rank), 0)
@@ -231,20 +247,15 @@
     order, rank = upper_left.shape[1], sketch_right.shape[1]
     bits = list(range(count.bit_length() - 1))
     near_first = bits
-    far_first = bits[:1] + bits[2:] + bits[1:2]
-    near = sum_rows(
-        jnp.concatenate(strips(upper_right, lower_right) + upper_strips(upper_left), axis=1),
-        near_first, me, count,
-    )
-    far = sum_rows(
-        jnp.concatenate(
-            strips(lower_left, sketch_right)
-            + strips(upper_left, sketch_left)
-            + upper_strips(lower_left),
-            axis=1,
-        ),
-        far_first, me, count,
-    )
+    far_first = bits[:1] + bits[2:3] + bits[1:2] + bits[3:]
+    near = jnp.concatenate(strips(upper_right, lower_right) + upper_strips(upper_left), axis=1)
+    far = jnp.concatenate(
+        strips(lower_left, sketch_right)
+        + strips(upper_left, sketch_left)
+        + upper_strips(lower_left),
+        axis=1,
+    )
+    near, far = sum_rows([near, far], [near_first, far_first], me, count)
     return tail(me, pairing, near, far, order, rank, half_rows, count)
 
 

time: 229 us -> 219 us (0.956)
  waiting for transfers between devices: 103 us -> 85.2 us
  other arithmetic: 10.4 us -> 14.5 us
  local copies, waits for them, and re-layouts: 8.73 us -> 11.2 us
    ppermute x16, waiting for transfers between devices: 103 us -> 85.2 us  [exchange(): lax.ppermute(value, 'cols', [(i, i ^ 1 << bit) for i in range(count)])]
    add x6, other arithmetic: 3.5 us -> 7.58 us  [sum_rows(): partials = [k + other.astype(F32) for k, other in zip(kept, others)]]
    convert_element_type x8, local copies, waits for them, and re-layouts: 3.72 us -> 6.88 us  [sum_rows(): lax.dynamic_slice_in_dim(partial, (1 - mine) * half, half, 0).astype(BF16)]
  transfers between devices with their start and end apart: 16 -> 16, of which waited for: 12 -> 12; matrix products, arithmetic and copies ran while one was open for 10% -> 12% of each run, Pallas kernels for 0% -> 0%
where the time goes in v3:
time: 219 us; the launch traced here: 217 us
  waiting for transfers between devices  85.2 us (39%)
  Pallas kernels  56.4 us (26%)
  matrix products  39 us (18%)
  other arithmetic  14.5 us (7%)
  local copies, waits for them, and re-layouts  11.2 us (5%)
  starting transfers between devices  9.99 us (5%)
    ppermute x16, waiting for transfers between devices, exchange(): lax.ppermute(value, 'cols', [(i, i ^ 1 << bit) for i in range(count)])  85.2 us
    pallas_call x1, Pallas kernels, tail(): pl.pallas_call(functools.partial(tail_kernel, half_rows=half_rows, units=...  56.4 us
    dot_general x20, matrix products, contract(): lax.dot_general(first, second, (((0,), (0,)), ((), ())), preferred_elemen...  39 us
    ppermute x16, starting transfers between devices, exchange(): lax.ppermute(value, 'cols', [(i, i ^ 1 << bit) for i in range(count)])  9.99 us
    add x6, other arithmetic, sum_rows(): partials = [k + other.astype(F32) for k, other in zip(kept, others)]  7.58 us
    convert_element_type x8, local copies, waits for them, and re-layouts, sum_rows(): lax.dynamic_slice_in_dim(partial, (1 - mine) * half, half, 0).astype(BF16)  6.88 us
    select_n x8, other arithmetic, sum_rows(): jnp.where(me >> bit & 1 == 0, jnp.concatenate([share, other], axis=0), jn...  6.82 us
  transfers between devices with their start and end apart: 16, of which 12 were waited for; matrix products, arithmetic and copies ran while one was open for 12% of the time, Pallas kernels for 0%

profile of v3, /device:TPU:29, one launch (start us, length us, event | category | flops | bytes accessed | tf_op | source)
XLA Modules:
  0.0 217.3 jit_solution(10898292028074649753)
XLA Ops:
  2.1 3.1 %convolution_dynamic-update-slice_fusion.13 = f32[256,5632]{1,0:T(8,128)} fusion(bf16[2400,384]{1,0:T(8,128)(2,1)S(1)} %copy-done, bf16[2400,1024]{1,0:T(8,128)(2,1)} %param.9), kind=kOutput, calls=%fused_computation.37 | convolution fusion | flops 471859200 | bytes 3465216 | tf_op jit(solution)/shard_map/dot_general | solution.py:17
  5.2 2.9 %convolution_dynamic-update-slice_fusion.12 = f32[256,5632]{1,0:T(8,128)} fusion(f32[256,5632]{1,0:T(8,128)} %convolution_dynamic-update-slice_fusion.13, bf16[2400,384]{1,0:T(8,128)(2,1)S(1)} %copy-done, bf16[2400,1024]{1,0:T(8,128)(2,1)} %param.9), kind=kOutput, calls=%fused_computation.36 | convolution fusion | flops 471859200 | bytes 3465216 | tf_op jit(solution)/shard_map/dot_general | solution.py:17
  18.4 2.6 %convolution_dynamic-update-slice_fusion = f32[256,5632]{1,0:T(8,128)} fusion(f32[256,5632]{1,0:T(8,128)} %convolution_dynamic-update-slice_fusion.6, bf16[2400,1024]{1,0:T(8,128)(2,1)S(1)} %copy-done.4), kind=kOutput, calls=%fused_computation.17 | convolution fusion | flops 1258291200 | bytes 7192576 | tf_op jit(solution)/shard_map/dot_general | solution.py:17
  21.0 2.2 fusion.11
  26.1 3.2 %dynamic-slice_convert_fusion.1 = bf16[128,5632]{1,0:T(8,128)(2,1)} fusion(f32[256,5632]{1,0:T(8,128)} %convolution_dynamic-update-slice_fusion.14, s32[]{:T(128)S(6)} %select_n.109), kind=kLoop, calls=%fused_computation.9 | loop fusion | bytes 2883588 | tf_op jit(solution)/shard_map/convert_element_type | solution.py:58
  30.1 4.7 %convolution_dynamic-update-slice_fusion.5 = f32[256,6656]{1,0:T(8,128)S(1)} fusion(bf16[2400,1024]{1,0:T(8,128)(2,1)} %param.10, bf16[2400,1024]{1,0:T(8,128)(2,1)} %param.8), kind=kOutput, calls=%fused_computation.22 | convolution fusion | flops 1258291200 | bytes 7192576 | tf_op jit(solution)/shard_map/dot_general | solution.py:17
  34.8 3.0 %convolution_dynamic-update-slice_fusion.4 = f32[256,6656]{1,0:T(8,128)S(1)} fusion(f32[256,6656]{1,0:T(8,128)S(1)} %convolution_dynamic-update-slice_fusion.5, bf16[2400,1024]{1,0:T(8,128)(2,1)S(1)} %bitcast.18, bf16[2400,1024]{1,0:T(8,128)(2,1)} %param.8), kind=kOutput, calls=%fused_computation.21 | convolution fusion | flops 1258291200 | bytes 7192576 | tf_op jit(solution)/shard_map/dot_general | solution.py:17
  45.3 2.8 %copy-done.6 = f32[256,6656]{1,0:T(8,128)} copy-done((f32[256,6656]{1,0:T(8,128)}, f32[256,6656]{1,0:T(8,128)S(1)}, u32[]{:S(2)}) %copy-start.6) | copy-done | bytes 6815768
  48.4 3.8 %convert_add_fusion.1 = f32[128,5632]{1,0:T(8,128)} fusion(bf16[128,5632]{1,0:T(8,128)(2,1)S(1)} %collective-permute-done.1, f32[256,5632]{1,0:T(8,128)} %convolution_dynamic-update-slice_fusion.14, s32[]{:T(128)S(6)} %select_n.108), kind=kLoop, calls=%fused_computation.8 | loop fusion | flops 1441792 | bytes 7208964 | tf_op jit(solution)/shard_map/add | solution.py:61
  52.1 2.3 %dynamic-slice_convert_fusion.3 = bf16[64,5632]{1,0:T(8,128)(2,1)} fusion(f32[128,5632]{1,0:T(8,128)} %convert_add_fusion.1, s32[]{:T(128)S(6)} %select_n.112), kind=kLoop, calls=%fused_computation.25 | loop fusion | bytes 1441796 | tf_op jit(solution)/shard_map/convert_element_type | solution.py:58
  57.6 17.1 %collective-permute-done.9 = bf16[64,5632]{1,0:T(8,128)(2,1)} collective-permute-done((bf16[64,5632]{1,0:T(8,128)(2,1)}, bf16[64,5632]{1,0:T(8,128)(2,1)}, u32[]{:S(2)}, u32[]{:S(2)}) %collective-permute-start.9) | collective-permute-done | bytes 720928 | tf_op jit(solution)/shard_map/ppermute | solution.py:41
  78.9 6.2 %collective-permute-done.10 = bf16[32,5632]{1,0:T(8,128)(2,1)S(1)} collective-permute-done((bf16[32,5632]{1,0:T(8,128)(2,1)S(1)}, bf16[32,5632]{1,0:T(8,128)(2,1)S(1)}, u32[]{:S(2)}, u32[]{:S(2)}) %collective-permute-start.10) | collective-permute-done | bytes 360480 | tf_op jit(solution)/shard_map/ppermute | solution.py:41
  87.9 14.3 %collective-permute-done.11 = bf16[16,5632]{1,0:T(8,128)(2,1)S(1)} collective-permute-done((bf16[16,5632]{1,0:T(8,128)(2,1)S(1)}, bf16[16,5632]{1,0:T(8,128)(2,1)S(1)}, u32[]{:S(2)}, u32[]{:S(2)}) %collective-permute-start.11) | collective-permute-done | bytes 180256 | tf_op jit(solution)/shard_map/ppermute | solution.py:41
  102.4 8.7 %collective-permute-done.4 = bf16[16,6656]{1,0:T(8,128)(2,1)S(1)} collective-permute-done((bf16[16,6656]{1,0:T(8,128)(2,1)S(1)}, bf16[16,6656]{1,0:T(8,128)(2,1)S(1)}, u32[]{:S(2)}, u32[]{:S(2)}) %collective-permute-start.4) | collective-permute-done | bytes 213024 | tf_op jit(solution)/shard_map/ppermute | solution.py:41
  111.2 6.0 %collective-permute-done.12 = bf16[16,5632]{1,0:T(8,128)(2,1)S(1)} collective-permute-done((bf16[16,5632]{1,0:T(8,128)(2,1)S(1)}, bf16[16,5632]{1,0:T(8,128)(2,1)S(1)}, u32[]{:S(2)}, u32[]{:S(2)}) %collective-permute-start.12) | collective-permute-done | bytes 180256 | tf_op jit(solution)/shard_map/ppermute | solution.py:41
  117.4 4.3 %collective-permute-done.5 = bf16[16,6656]{1,0:T(8,128)(2,1)S(1)} collective-permute-done((bf16[16,6656]{1,0:T(8,128)(2,1)S(1)}, bf16[16,6656]{1,0:T(8,128)(2,1)S(1)}, u32[]{:S(2)}, u32[]{:S(2)}) %collective-permute-start.5) | collective-permute-done | bytes 213024 | tf_op jit(solution)/shard_map/ppermute | solution.py:41
  121.9 3.1 %collective-permute-done.13 = bf16[32,5632]{1,0:T(8,128)(2,1)S(1)} collective-permute-done((bf16[32,5632]{1,0:T(8,128)(2,1)S(1)}, bf16[32,5632]{1,0:T(8,128)(2,1)S(1)}, u32[]{:S(2)}, u32[]{:S(2)}) %collective-permute-start.13) | collective-permute-done | bytes 360480 | tf_op jit(solution)/shard_map/ppermute | solution.py:41
  125.2 6.7 %collective-permute-done.6 = bf16[32,6656]{1,0:T(8,128)(2,1)S(1)} collective-permute-done((bf16[32,6656]{1,0:T(8,128)(2,1)S(1)}, bf16[32,6656]{1,0:T(8,128)(2,1)S(1)}, u32[]{:S(2)}, u32[]{:S(2)}) %collective-permute-start.6) | collective-permute-done | bytes 426016 | tf_op jit(solution)/shard_map/ppermute | solution.py:41
  132.1 15.2 %collective-permute-done.14 = bf16[64,5632]{1,0:T(8,128)(2,1)S(1)} collective-permute-done((bf16[64,5632]{1,0:T(8,128)(2,1)S(1)}, bf16[64,5632]{1,0:T(8,128)(2,1)S(1)}, u32[]{:S(2)}, u32[]{:S(2)}) %collective-permute-start.14) | collective-permute-done | bytes 720928 | tf_op jit(solution)/shard_map/ppermute | solution.py:41
  147.6 2.3 %collective-permute-start.15 = (bf16[128,5632]{1,0:T(8,128)(2,1)S(1)}, bf16[128,5632]{1,0:T(8,128)(2,1)}, u32[]{:S(2)}, u32[]{:S(2)}) collective-permute-start(bf16[128,5632]{1,0:T(8,128)(2,1)S(1)} %maximum_select_fusion.3), channel_id=1, source_target_pairs={{0,1},{1,0},{2,3},{3,2},{4,5},{5,4},{6,7},{7,6},{8,9},{9,8},{10,11... | collective-permute-start | bytes 4325384 | tf_op jit(solution)/shard_map/ppermute | solution.py:41
  150.2 3.6 %collective-permute-start.8 = (bf16[128,6656]{1,0:T(8,128)(2,1)S(1)}, bf16[128,6656]{1,0:T(8,128)(2,1)}, u32[]{:S(2)}, u32[]{:S(2)}) collective-permute-start(bf16[128,6656]{1,0:T(8,128)(2,1)S(1)} %maximum_select_fusion.2), channel_id=1, source_target_pairs={{0,1},{1,0},{2,3},{3,2},{4,5},{5,4},{6,7},{7,6},{8,9},{9,8},{10,11... | collective-permute-start | bytes 5111816 | tf_op jit(solution)/shard_map/ppermute | solution.py:41
  153.8 2.2 %maximum_select_fusion.1.far_ref = bf16[256,5632]{1,0:T(8,128)(2,1)S(1)} fusion(bf16[128,5632]{1,0:T(8,128)(2,1)} %collective-permute-done.15, bf16[128,5632]{1,0:T(8,128)(2,1)S(1)} %maximum_select_fusion.3, pred[]{:T(512)S(6)} %eq.16), kind=kLoop, calls=%fused_computation.7 | loop fusion | flops 12976128 | bytes 5767169 | tf_op jit(solution)/shard_map/jit(_where)/select_n | solution.py:66
  157.2 3.7 %maximum_select_fusion.near_ref = bf16[256,6656]{1,0:T(8,128)(2,1)} fusion(bf16[128,6656]{1,0:T(8,128)(2,1)} %collective-permute-done.8, bf16[128,6656]{1,0:T(8,128)(2,1)S(1)} %maximum_select_fusion.2, pred[]{:T(512)S(6)} %eq.16), kind=kLoop, calls=%fused_computation.4 | loop fusion | flops 15335424 | bytes 6815745 | tf_op jit(solution)/shard_map/jit(_where)/select_n | solution.py:66
  160.9 56.4 %shard_map.86 = (f32[64,384]{1,0:T(8,128)}, f32[64,384]{1,0:T(8,128)}) custom-call(s32[1]{0:T(128)} %bitcast.where_ref, s32[16]{0:T(128)S(1)} %copy-done.2, bf16[256,6656]{1,0:T(8,128)(2,1)} %maximum_select_fusion.near_ref, bf16[256,5632]{1,0:T(8,128)(2,1)S(1)} %maximum_select_fusion.1.far_ref), custom_call_target="tpu_custom_call" | custom-call | tf_op jit(solution)/shard_map/pallas_call | solution.py:226
  (84 shorter events, 35.7 us)
Async XLA Ops:
  2.1 6.0 %copy-start.4 = (bf16[2400,1024]{1,0:T(8,128)(2,1)S(1)}, bf16[2400,1024]{1,0:T(8,128)(2,1)}, u32[]{:S(2)}) copy-start(bf16[2400,1024]{1,0:T(8,128)(2,1)} %param.9) | copy-start | bytes 14745604
  24.9 12.9 %slice-start.4 = ((s8[4915200]{0:T(1024)(128)(4,1)}), s8[720896]{0:T(1024)(128)(4,1)S(1)}, s32[]{:S(2)}) async-start(s8[4915200]{0:T(1024)(128)(4,1)} %bitcast.19), calls=%async_computation.4 | async-start | bytes 1441792
  26.1 8.6 %slice-start.2 = ((s8[4915200]{0:T(1024)(128)(4,1)}), s8[4194304]{0:T(1024)(128)(4,1)S(1)}, s32[]{:S(2)}) async-start(s8[4915200]{0:T(1024)(128)(4,1)} %bitcast.17), calls=%async_computation.2 | async-start | bytes 8388608
  29.4 5.4 %slice-start.3 = ((s8[4915200]{0:T(1024)(128)(4,1)}), s8[720896]{0:T(1024)(128)(4,1)S(1)}, s32[]{:S(2)}) async-start(s8[4915200]{0:T(1024)(128)(4,1)} %bitcast.17), calls=%async_computation.3 | async-start | bytes 1441792
  29.4 8.5 %slice-start.5 = ((s8[4915200]{0:T(1024)(128)(4,1)}), s8[4194304]{0:T(1024)(128)(4,1)S(1)}, s32[]{:S(2)}) async-start(s8[4915200]{0:T(1024)(128)(4,1)} %bitcast.19), calls=%async_computation.5 | async-start | bytes 8388608
  29.4 19.0 %collective-permute-start.1 = (bf16[128,5632]{1,0:T(8,128)(2,1)}, bf16[128,5632]{1,0:T(8,128)(2,1)S(1)}, u32[]{:S(2)}, u32[]{:S(2)}) collective-permute-start(bf16[128,5632]{1,0:T(8,128)(2,1)} %dynamic-slice_convert_fusion.1), channel_id=1, source_target_pairs={{0,1},{1,0},{2,3},{3,2},{4,5},{5,4},{6,7},{7,6},{8,9},{9,8},{10,11... | collective-permute-start | bytes 4325384 | tf_op jit(solution)/shard_map/ppermute | solution.py:41
  48.2 6.2 %collective-permute-start = (bf16[128,6656]{1,0:T(8,128)(2,1)S(1)}, bf16[128,6656]{1,0:T(8,128)(2,1)}, u32[]{:S(2)}, u32[]{:S(2)}) collective-permute-start(bf16[128,6656]{1,0:T(8,128)(2,1)S(1)} %dynamic-slice_convert_fusion), channel_id=1, source_target_pairs={{0,1},{1,0},{2,3},{3,2},{4,5},{5,4},{6,7},{7,6},{8,9},{9,8},{10,11... | collective-permute-start | bytes 5111816 | tf_op jit(solution)/shard_map/ppermute | solution.py:41
  48.3 6.1 %copy-start.7 = (f32[256,6656]{1,0:T(8,128)S(1)}, f32[256,6656]{1,0:T(8,128)}, u32[]{:S(2)}) copy-start(f32[256,6656]{1,0:T(8,128)} %copy-done.6) | copy-start | bytes 20447236
  57.2 17.5 %collective-permute-start.9 = (bf16[64,5632]{1,0:T(8,128)(2,1)}, bf16[64,5632]{1,0:T(8,128)(2,1)}, u32[]{:S(2)}, u32[]{:S(2)}) collective-permute-start(bf16[64,5632]{1,0:T(8,128)(2,1)} %dynamic-slice_convert_fusion.3), channel_id=1, source_target_pairs={{0,4},{1,5},{2,6},{3,7},{4,0},{5,1},{6,2},{7,3},{8,12},{9,13},{10,... | collective-permute-start | bytes 2162696 | tf_op jit(solution)/shard_map/ppermute | solution.py:41
  57.3 19.9 %collective-permute-start.2 = (bf16[64,6656]{1,0:T(8,128)(2,1)}, bf16[64,6656]{1,0:T(8,128)(2,1)S(1)}, u32[]{:S(2)}, u32[]{:S(2)}) collective-permute-start(bf16[64,6656]{1,0:T(8,128)(2,1)} %dynamic-slice_convert_fusion.2), channel_id=1, source_target_pairs={{0,2},{1,3},{2,0},{3,1},{4,6},{5,7},{6,4},{7,5},{8,10},{9,11},{10,... | collective-permute-start | bytes 2555912 | tf_op jit(solution)/shard_map/ppermute | solution.py:41
  76.5 8.6 %collective-permute-start.10 = (bf16[32,5632]{1,0:T(8,128)(2,1)S(1)}, bf16[32,5632]{1,0:T(8,128)(2,1)S(1)}, u32[]{:S(2)}, u32[]{:S(2)}) collective-permute-start(bf16[32,5632]{1,0:T(8,128)(2,1)S(1)} %dynamic-slice_convert_fusion.5), channel_id=1, source_target_pairs={{0,2},{1,3},{2,0},{3,1},{4,6},{5,7},{6,4},{7,5},{8,10},{9,11},{10,... | collective-permute-start | bytes 1081352 | tf_op jit(solution)/shard_map/ppermute | solution.py:41
  77.5 9.7 %collective-permute-start.3 = (bf16[32,6656]{1,0:T(8,128)(2,1)S(1)}, bf16[32,6656]{1,0:T(8,128)(2,1)S(1)}, u32[]{:S(2)}, u32[]{:S(2)}) collective-permute-start(bf16[32,6656]{1,0:T(8,128)(2,1)S(1)} %dynamic-slice_convert_fusion.4), channel_id=1, source_target_pairs={{0,4},{1,5},{2,6},{3,7},{4,0},{5,1},{6,2},{7,3},{8,12},{9,13},{10,... | collective-permute-start | bytes 1277960 | tf_op jit(solution)/shard_map/ppermute | solution.py:41
  85.3 17.0 %collective-permute-start.11 = (bf16[16,5632]{1,0:T(8,128)(2,1)S(1)}, bf16[16,5632]{1,0:T(8,128)(2,1)S(1)}, u32[]{:S(2)}, u32[]{:S(2)}) collective-permute-start(bf16[16,5632]{1,0:T(8,128)(2,1)S(1)} %dynamic-slice_convert_fusion.7), channel_id=1, source_target_pairs={{0,8},{1,9},{2,10},{3,11},{4,12},{5,13},{6,14},{7,15},{8,0},{9,1},... | collective-permute-start | bytes 540680 | tf_op jit(solution)/shard_map/ppermute | solution.py:41
  87.3 23.7 %collective-permute-start.4 = (bf16[16,6656]{1,0:T(8,128)(2,1)S(1)}, bf16[16,6656]{1,0:T(8,128)(2,1)S(1)}, u32[]{:S(2)}, u32[]{:S(2)}) collective-permute-start(bf16[16,6656]{1,0:T(8,128)(2,1)S(1)} %dynamic-slice_convert_fusion.6), channel_id=1, source_target_pairs={{0,8},{1,9},{2,10},{3,11},{4,12},{5,13},{6,14},{7,15},{8,0},{9,1},... | collective-permute-start | bytes 638984 | tf_op jit(solution)/shard_map/ppermute | solution.py:41
  102.3 14.9 %collective-permute-start.12 = (bf16[16,5632]{1,0:T(8,128)(2,1)S(1)}, bf16[16,5632]{1,0:T(8,128)(2,1)S(1)}, u32[]{:S(2)}, u32[]{:S(2)}) collective-permute-start(bf16[16,5632]{1,0:T(8,128)(2,1)S(1)} %add_convert_fusion.1), channel_id=1, source_target_pairs={{0,8},{1,9},{2,10},{3,11},{4,12},{5,13},{6,14},{7,15},{8,0},{9,1},... | collective-permute-start | bytes 540680 | tf_op jit(solution)/shard_map/ppermute | solution.py:41
  111.1 10.7 %collective-permute-start.5 = (bf16[16,6656]{1,0:T(8,128)(2,1)S(1)}, bf16[16,6656]{1,0:T(8,128)(2,1)S(1)}, u32[]{:S(2)}, u32[]{:S(2)}) collective-permute-start(bf16[16,6656]{1,0:T(8,128)(2,1)S(1)} %add_convert_fusion), channel_id=1, source_target_pairs={{0,8},{1,9},{2,10},{3,11},{4,12},{5,13},{6,14},{7,15},{8,0},{9,1},... | collective-permute-start | bytes 638984 | tf_op jit(solution)/shard_map/ppermute | solution.py:41
  117.2 7.8 %collective-permute-start.13 = (bf16[32,5632]{1,0:T(8,128)(2,1)S(1)}, bf16[32,5632]{1,0:T(8,128)(2,1)S(1)}, u32[]{:S(2)}, u32[]{:S(2)}) collective-permute-start(bf16[32,5632]{1,0:T(8,128)(2,1)S(1)} %maximum_select_fusion.7), channel_id=1, source_target_pairs={{0,2},{1,3},{2,0},{3,1},{4,6},{5,7},{6,4},{7,5},{8,10},{9,11},{10,... | collective-permute-start | bytes 1081352 | tf_op jit(solution)/shard_map/ppermute | solution.py:41
  121.8 10.1 %collective-permute-start.6 = (bf16[32,6656]{1,0:T(8,128)(2,1)S(1)}, bf16[32,6656]{1,0:T(8,128)(2,1)S(1)}, u32[]{:S(2)}, u32[]{:S(2)}) collective-permute-start(bf16[32,6656]{1,0:T(8,128)(2,1)S(1)} %maximum_select_fusion.6), channel_id=1, source_target_pairs={{0,4},{1,5},{2,6},{3,7},{4,0},{5,1},{6,2},{7,3},{8,12},{9,13},{10,... | collective-permute-start | bytes 1277960 | tf_op jit(solution)/shard_map/ppermute | solution.py:41
  125.1 22.2 %collective-permute-start.14 = (bf16[64,5632]{1,0:T(8,128)(2,1)S(1)}, bf16[64,5632]{1,0:T(8,128)(2,1)S(1)}, u32[]{:S(2)}, u32[]{:S(2)}) collective-permute-start(bf16[64,5632]{1,0:T(8,128)(2,1)S(1)} %maximum_select_fusion.5), channel_id=1, source_target_pairs={{0,4},{1,5},{2,6},{3,7},{4,0},{5,1},{6,2},{7,3},{8,12},{9,13},{10,... | collective-permute-start | bytes 2162696 | tf_op jit(solution)/shard_map/ppermute | solution.py:41
  132.0 17.8 %collective-permute-start.7 = (bf16[64,6656]{1,0:T(8,128)(2,1)S(1)}, bf16[64,6656]{1,0:T(8,128)(2,1)S(1)}, u32[]{:S(2)}, u32[]{:S(2)}) collective-permute-start(bf16[64,6656]{1,0:T(8,128)(2,1)S(1)} %maximum_select_fusion.4), channel_id=1, source_target_pairs={{0,2},{1,3},{2,0},{3,1},{4,6},{5,7},{6,4},{7,5},{8,10},{9,11},{10,... | collective-permute-start | bytes 2555912 | tf_op jit(solution)/shard_map/ppermute | solution.py:41
  147.6 6.2 %collective-permute-start.15 = (bf16[128,5632]{1,0:T(8,128)(2,1)S(1)}, bf16[128,5632]{1,0:T(8,128)(2,1)}, u32[]{:S(2)}, u32[]{:S(2)}) collective-permute-start(bf16[128,5632]{1,0:T(8,128)(2,1)S(1)} %maximum_select_fusion.3), channel_id=1, source_target_pairs={{0,1},{1,0},{2,3},{3,2},{4,5},{5,4},{6,7},{7,6},{8,9},{9,8},{10,11... | collective-permute-start | bytes 4325384 | tf_op jit(solution)/shard_map/ppermute | solution.py:41
  150.2 7.0 %collective-permute-start.8 = (bf16[128,6656]{1,0:T(8,128)(2,1)S(1)}, bf16[128,6656]{1,0:T(8,128)(2,1)}, u32[]{:S(2)}, u32[]{:S(2)}) collective-permute-start(bf16[128,6656]{1,0:T(8,128)(2,1)S(1)} %maximum_select_fusion.2), channel_id=1, source_target_pairs={{0,1},{1,0},{2,3},{3,2},{4,5},{5,4},{6,7},{7,6},{8,9},{9,8},{10,11... | collective-permute-start | bytes 5111816 | tf_op jit(solution)/shard_map/ppermute | solution.py:41
  156.0 4.8 %copy-start.2 = (s32[16]{0:T(128)S(1)}, s32[16]{0:T(128)}, u32[]{:S(2)}) copy-start(s32[16]{0:T(128)} %pairing_ref.1) | copy-start | bytes 196
  157.2 60.1 %copy-start.1 = (bf16[2400,384]{1,0:T(8,128)(2,1)S(1)}, bf16[2400,384]{1,0:T(8,128)(2,1)}, u32[]{:S(2)}) copy-start(bf16[2400,384]{1,0:T(8,128)(2,1)} %param.11) | copy-start | bytes 5529604
  (6 other events, 15.9 us)
